TPU v7x, 32 devices: a whole 2x2x4 slice. The times are simulated.
32 devices in a mesh: survey: 2 (over x), pole: 2 (over core), space: 8 (over z, y).
Axes of the slice: x: 2, y: 2, z: 4, core: 2. Of those that a mesh axis runs over, the one named last changes fastest.
Arguments:
- conductivity: float32 [64, 64, 128], P(('survey', 'space')), parts along dimension 0, may hold values from 0.3 to 9
- source_field: float32 [3, 64, 64, 128], P(None, ('survey', 'space')), parts along dimension 1, may hold values from -6 to 6
- shifts: float32 [8], replicated, may hold values from 1 to 10
- residues: float32 [12, 8], replicated, may hold values from -4 to 4
- receivers: int32 [512], P('survey'), parts along dimension 0, may hold values from 0 to 262143
Outputs:
- gated_field: float32 [12, 3, 64, 64, 128], P(None, None, ('survey', 'space'), 'pole'), parts along dimension 2
- traces: float32 [12, 3, 512], P(None, None, 'survey'), parts along dimension 2
There are 2 independent parts, one for each index of `survey`. A program takes and returns all parts, laid end to end along the dimension named above; an argument that names none is the same for every part. Nothing has to cross between parts.
All inputs are finite; a program needn't handle non-finite values.
Results may differ from a plain program's by a relative error of at most 0.000084.
Values sent between devices are 32-bit elements; how exact they have to be, the bound alone decides.
No kernel may reach another device: no remote copies, remote signals or barrier semaphores. Data moves between devices by JAX's collectives and lax.ppermute only.
A program may use at most 128 MiB of HBM per device.

v0:
```python
import functools

import jax
import jax.numpy as jnp
from jax import lax
from jax.experimental import pallas as pl
from jax.experimental.pallas import tpu as pltpu
from jax.sharding import PartitionSpec as P

MID = 4.65
WORDS = 10
SLOTS = 32
TILE = 8
VMEM = pl.BlockSpec(memory_space=pltpu.VMEM)
SMEM = pl.BlockSpec(memory_space=pltpu.SMEM)
PARAMS = pltpu.CompilerParams(vmem_limit_bytes=48 * 1024 * 1024)


def sub_next(v):
    return pltpu.roll(v, v.shape[0] - 1, 0)


def sub_prev(v):
    return pltpu.roll(v, 1, 0)


def lanes_of(v):
    return lax.broadcasted_iota(jnp.int32, v.shape, 1)


def rows_of(v):
    return lax.broadcasted_iota(jnp.int32, v.shape, 0)


def lane_next(v):
    return jnp.where(lanes_of(v) == v.shape[1] - 1, 0.0, pltpu.roll(v, v.shape[1] - 1, 1))


def lane_prev(v, first):
    return jnp.where(lanes_of(v) == 0, first, pltpu.roll(v, 1, 1))


def part_keep(core):
    row = lax.broadcasted_iota(jnp.int32, (TILE, 128), 0)
    return jnp.where(core == 0, (row < 5).astype(jnp.float32), (row >= 5).astype(jnp.float32))


def own_rows(half, core):
    return pl.ds(pl.multiple_of(core * half, TILE), half)


def extra_rows(half, core):
    return pl.ds(pl.multiple_of(half - core * TILE, TILE), TILE)


def to_front(tile, core):
    return jnp.where(core == 0, tile, pltpu.roll(tile, 3, 0))


def from_front(tile, core):
    tile = jnp.where(rows_of(tile) < 3, tile, 0.0)
    return jnp.where(core == 0, tile, pltpu.roll(tile, TILE - 3, 0))


def pack_extras(near, far, ends):
    row = rows_of(ends)
    spare = [
        pltpu.roll(far[0], 6, 0),
        pltpu.roll(far[1], 6, 0),
        jnp.where(row == 6, pltpu.roll(far[0], 4, 0), pltpu.roll(far[1], 5, 0)),
        pltpu.roll(ends, 6, 0),
    ]
    return [
        jnp.where(
            row < 3,
            near[2 * at],
            jnp.where(row < 6, pltpu.roll(near[2 * at + 1], 3, 0), spare[at]),
        )
        for at in range(4)
    ]


def unpack_near(tiles, at, core):
    tile = tiles[at // 2]
    return from_front(pltpu.roll(tile, TILE - 3, 0) if at % 2 else tile, core)


def unpack_far(tiles, at, core):
    last = pltpu.roll(tiles[2], 4 - at, 0)
    return from_front(jnp.where(rows_of(last) < 2, pltpu.roll(tiles[at], 2, 0), last), core)


def send_kernel(cond_hbm, src_hbm, first_ref, second_ref, cond_out, field_out, ends_ref, cond_ref, src_ref, sems):
    core = lax.axis_index("pole")
    odd = lax.rem(lax.axis_index("space"), 2)
    layers, rows, _ = cond_ref.shape
    half = rows // 2
    own, extra = own_rows(half, core), extra_rows(half, core)
    keep = part_keep(core)
    copies = [pltpu.make_async_copy(cond_hbm, cond_ref, sems.at[0])] + [
        pltpu.make_async_copy(src_hbm.at[c], src_ref.at[c], sems.at[1 + c]) for c in range(3)
    ]
    for copy in copies:
        copy.start()
    for copy in copies:
        copy.wait()

    conds, fields = [], []
    for layer in range(layers):
        cond = jnp.concatenate([cond_ref[layer, own, :], cond_ref[layer, extra, :] * keep], axis=0)
        field = [
            cond * jnp.concatenate([src_ref[c, layer, own, :], src_ref[c, layer, extra, :]], axis=0)
            for c in range(3)
        ]
        cond_out[layer] = cond
        for c in range(3):
            field_out[layer, c] = field[c]
        conds.append(cond)
        fields.append(field)

    top = jnp.max(jnp.max(cond_ref[...], axis=0), axis=0, keepdims=True)
    low = jnp.max(-jnp.min(cond_ref[...], axis=0), axis=0, keepdims=True)
    row = lax.broadcasted_iota(jnp.int32, (TILE, 128), 0)
    ends = jnp.where(row == 0, top, low)
    ends_ref[...] = ends
    for upward in (True, False):
        near = [layers - 1, layers - 2] if upward else [0, 1]
        fx, fy, fz = fields[layers - 3 if upward else 2]
        far = [fy + sub_next(fx) - fx, fz + lane_next(fx) - fx] if upward else [fy, fz]
        blocks = [v for layer in near for v in (*fields[layer], conds[layer])] + far
        edges = [to_front(block[half:], core) for block in blocks]
        pairs = pack_extras(edges[:8], edges[8:], ends)

        def write(out_ref):
            for at, block in enumerate(blocks):
                out_ref[at * half : (at + 1) * half, :] = block[:half]
            base = len(blocks) * half
            for at, pair in enumerate(pairs):
                out_ref[base + at * TILE : base + (at + 1) * TILE, :] = pair

        with_first = odd == 0 if upward else odd == 1

        @pl.when(with_first)
        def _():
            write(first_ref)

        @pl.when(jnp.logical_not(with_first))
        def _():
            write(second_ref)


def list_kernel(rec_ref, shifts_ref, res_ref, list_ref, par_ref, square, *, layers, rows, depth):
    core = lax.axis_index("pole")
    base = lax.axis_index("space") * layers
    half = rows // 2
    total = rec_ref.shape[0]

    def step(at, count):
        cell = rec_ref[at]
        x = lax.div(cell, rows * depth) - base
        y = lax.rem(lax.div(cell, depth), rows) - core * half
        owned = (x >= 0) & (x < layers) & (y >= 0) & (y < half)
        start = x * (SLOTS * half) + y
        list_ref[count] = (start * depth + lax.rem(cell, depth)) * total + at
        return count + owned.astype(jnp.int32)

    list_ref[total] = lax.fori_loop(0, total, step, jnp.int32(0), unroll=8)
    poles, gates = res_ref.shape
    square[...] = jnp.zeros_like(square)
    square[:poles, :gates] = res_ref[...]
    par_ref[...] = jnp.zeros_like(par_ref)
    par_ref[TILE : TILE + gates, :poles] = square[...].T[:gates, :poles]
    par_ref[:1, :poles] = shifts_ref[...]


def curl_curl(get_u, get, layers, put, half, trimmed=False):
    first = layers[0]
    u_y, u_z = get_u(first - 1)
    _, g, e = get(first, (1, 2))
    prev_z, prev_y = g - u_y, u_z - e
    for layer in layers:
        f, g, e = get(layer, (0, 1, 2))
        _, g_up, e_up = get(layer + 1, (1, 2))
        h_z = g_up - (g + (sub_next(f) - f))
        h_y = (e + (lane_next(f) - f)) - e_up
        h_x = (sub_next(e) - e) - (lane_next(g) - g)
        out_x = (h_z - sub_prev(h_z)) + (lane_prev(h_y, f) - h_y) - 8.0 * f
        out_y = (h_x - lane_prev(h_x, -g)) + (prev_z - h_z) - 8.0 * g
        out_z = (h_y - prev_y) + (sub_prev(h_x) - h_x) - 8.0 * e
        prev_z, prev_y = h_z, h_y
        put(layer, (out_x, out_y, out_z))


def basis_kernel(
    cond_ref, field_ref, ends_ref, first_ref, second_ref, list_hbm,
    bas_ref, sel_ref,
    sig, low3, high3, t00, t10, t11, t20, t21, t22, list_ref, list_sem,
):
    core = lax.axis_index("pole")
    place = lax.axis_index("space")
    odd = lax.rem(place, 2)
    layers, reach, depth = cond_ref.shape
    half = reach - TILE
    keep = part_keep(core)
    list_copy = pltpu.make_async_copy(list_hbm, list_ref, list_sem)
    list_copy.start()
    low_ok = (place > 0).astype(jnp.float32)
    high_ok = (place < lax.axis_size("space") - 1).astype(jnp.float32)

    def received(upward, at):
        part = pl.ds(at * half, half)
        from_first = odd == 1 if upward else odd == 0
        return jnp.where(from_first, first_ref[part, :], second_ref[part, :])

    def received_tile(upward, at):
        part = pl.ds(10 * half + at * TILE, TILE)
        from_first = odd == 1 if upward else odd == 0
        return jnp.where(from_first, first_ref[part, :], second_ref[part, :])

    for layer in range(layers):
        moved = cond_ref[layer] - MID
        sig[layer + 2] = moved
        for c in range(3):
            field = field_ref[layer, c]
            t00[layer + 2, c] = field
            t11[layer + 2, c] = moved * field
    for upward in (True, False):
        tiles = [received_tile(upward, at) for at in range(4)]
        for distance in (1, 2):
            slot = 2 - distance if upward else layers + 1 + distance
            base = (distance - 1) * 4
            moved = jnp.concatenate(
                [received(upward, base + 3), unpack_near(tiles, base + 3, core)], axis=0
            ) - MID
            sig[slot] = moved
            for c in range(3):
                field = jnp.concatenate(
                    [received(upward, base + c), unpack_near(tiles, base + c, core)], axis=0
                )
                t00[slot, c] = field
                t11[slot, c] = moved * field
        far = low3 if upward else high3
        for at in range(2):
            far[at] = jnp.concatenate(
                [received(upward, 8 + at), unpack_far(tiles, at, core)], axis=0
            )

    def sums(ref):
        def get_u(slot):
            f, g, e = ref[slot, 0], ref[slot, 1], ref[slot, 2]
            return g + (sub_next(f) - f), e + (lane_next(f) - f)

        return get_u

    def reader(ref):
        def get(slot, which):
            return [ref[slot, c] if c in which else None for c in range(3)]

        return get

    def inside(slot, value):
        value = jnp.concatenate([value[:half], value[half:] * keep], axis=0)
        if slot < 2:
            return value * low_ok
        if slot > layers + 1:
            return value * high_ok
        return value

    def get_b(slot, which):
        if slot > layers + 3:
            return None, high3[0], high3[1]
        return [t00[slot, c] if c in which else None for c in range(3)]

    def put_10(slot, out):
        for c in range(3):
            t10[slot, c] = inside(slot, out[c])

    curl_curl(lambda slot: (low3[0], low3[1]), get_b, list(range(layers + 4)), put_10, half)

    def put_20(slot, out):
        for c in range(3):
            t20[slot, c] = inside(slot, out[c])

    def put_21(slot, out):
        for c in range(3):
            t21[slot, c] = inside(slot, out[c]) + sig[slot] * t10[slot, c]
            t22[slot, c] = sig[slot] * t11[slot, c]

    middle = list(range(1, layers + 3))
    curl_curl(sums(t10), reader(t10), middle, put_20, half)
    curl_curl(sums(t11), reader(t11), middle, put_21, half)

    def store(word, slot, c, value):
        base = ((slot - 2) * SLOTS + word * 3 + c) * half
        bas_ref[base : base + half, :] = value

    inner = list(range(2, layers + 2))
    for slot in inner:
        for c in range(3):
            for word, ref in enumerate((t00, t10, t11, t20, t21, t22)):
                store(word, slot, c, ref[slot, c, :half, :])
            store(9, slot, c, sig[slot, :half, :] * t22[slot, c, :half, :])
        for spare in range(WORDS * 3, SLOTS):
            base = ((slot - 2) * SLOTS + spare) * half
            bas_ref[base : base + half, :] = jnp.zeros((half, depth), jnp.float32)

    def put_3(word, before):
        def put(slot, out):
            for c in range(3):
                value = out[c][:half]
                if before is not None:
                    value = value + sig[slot, :half, :] * before[slot, c, :half, :]
                store(word, slot, c, value)

        return put

    curl_curl(sums(t20), reader(t20), inner, put_3(6, None), half)
    curl_curl(sums(t21), reader(t21), inner, put_3(7, t20), half)
    curl_curl(sums(t22), reader(t22), inner, put_3(8, t21), half)

    groups = sel_ref.shape[0]
    for group in range(groups):
        sel_ref[group, :SLOTS, :] = jnp.zeros((SLOTS, depth), jnp.float32)
    tile = first_ref[10 * half + 3 * TILE : 10 * half + 4 * TILE, :]
    row = lax.broadcasted_iota(jnp.int32, (TILE, 128), 0)
    ends = jnp.maximum(ends_ref[...], jnp.where(row == 0, tile[6:7], tile[7:8]))
    for group in range(groups):
        sel_ref[group, SLOTS:, :] = ends

    lane = lax.broadcasted_iota(jnp.int32, (SLOTS, depth), 1)

    total = list_ref.shape[0] - 1
    list_copy.wait()

    def pick(at, carry):
        code = list_ref[at]
        which = lax.rem(code, total)
        cell = lax.div(code, total)
        z = lax.rem(cell, depth)
        block = bas_ref[pl.ds(lax.div(cell, depth), SLOTS, stride=half), :]
        target = lax.rem(which, 128)
        group = lax.div(which, 128)
        block = pltpu.roll(block, lax.rem(target - z + 128, 128), 1)
        sel_ref[group, :SLOTS, :] = jnp.where(lane == target, block, sel_ref[group, :SLOTS, :])
        return carry

    lax.fori_loop(0, list_ref[total], pick, 0)


def weights(ends_ref, par_ref, out_ref, gates, poles):
    upper = jnp.max(ends_ref[0, SLOTS : SLOTS + 1, :], axis=1, keepdims=True)
    lower = -jnp.max(ends_ref[0, SLOTS + 1 : SLOTS + 2, :], axis=1, keepdims=True)
    shift = jnp.where(lax.broadcasted_iota(jnp.int32, (1, 128), 1) < poles, par_ref[:1, :], 1.0)
    low_end = shift * lower
    high_end = 16.0 + shift * upper
    center = (high_end + low_end) / 2.0
    spread = (high_end - low_end) / 2.0
    scaled = center / spread
    residual = [jnp.ones_like(shift)]
    direction = [1.0 / center]
    ratio = 1.0 / scaled
    total = list(direction)
    for _ in range(3):
        applied = [center * d for d in direction] + [jnp.zeros_like(shift)]
        for at, d in enumerate(direction):
            applied[at + 1] = applied[at + 1] + spread * d
        residual = [
            (residual[at] if at < len(residual) else 0.0) - a for at, a in enumerate(applied)
        ]
        ratio_new = 1.0 / (2.0 * scaled - ratio)
        grown = [(2.0 * ratio_new / spread) * r for r in residual]
        direction = [
            g + ratio_new * ratio * direction[at] if at < len(direction) else g
            for at, g in enumerate(grown)
        ]
        ratio = ratio_new
        total = [
            d + total[at] if at < len(total) else d for at, d in enumerate(direction)
        ]
    offset = shift * (MID - (upper + lower) / 2.0)
    inverse = 1.0 / spread
    y0, y1, y2, y3 = total
    y1 = y1 * inverse
    y2 = y2 * inverse * inverse
    y3 = y3 * inverse * inverse * inverse
    powers = [
        y0 + offset * (y1 + offset * (y2 + offset * y3)),
        y1 + offset * (2.0 * y2 + 3.0 * offset * y3),
        y2 + 3.0 * offset * y3,
        y3,
    ]
    word = 0
    res = par_ref[TILE : TILE + gates, :]
    for m in range(4):
        term = powers[m]
        for _ in range(m + 1):
            column = jnp.sum(res * term, axis=1, keepdims=True)
            out_ref[word, : res.shape[0], :] = jnp.broadcast_to(column, (res.shape[0], 128))
            term = term * shift
            word += 1


def combine(w_ref, bas_ref, out_ref, gates):
    half = bas_ref.shape[2]
    for c in range(3):
        for top in range(0, half, TILE):
            terms = [bas_ref[0, word * 3 + c, top : top + TILE, :] for word in range(WORDS)]
            for g in range(gates):
                total = w_ref[0, g : g + 1, :] * terms[0]
                for word in range(1, WORDS):
                    total = total + w_ref[word, g : g + 1, :] * terms[word]
                out_ref[g, c, 0, top : top + TILE, :] = total


def gate_kernel(ends_ref, par_ref, bas_ref, out_ref, w_ref, *, poles):
    gates = out_ref.shape[0]

    @pl.when(pl.program_id(0) == 0)
    def _():
        weights(ends_ref, par_ref, w_ref, gates, poles)

    combine(w_ref, bas_ref, out_ref, gates)


def rest_kernel(w_ref, bas_ref, before_ref, out_ref):
    del before_ref
    combine(w_ref, bas_ref, out_ref, out_ref.shape[0])


def trace_kernel(w_ref, sel_ref, out_ref):
    gates = out_ref.shape[0]
    for group in range(sel_ref.shape[0]):
        for c in range(3):
            total = None
            for word in range(WORDS):
                at = word * 3 + c
                term = w_ref[word, :gates, :] * sel_ref[group, at : at + 1, :]
                total = term if total is None else total + term
            for g in range(gates):
                out_ref[g, c : c + 1, group * 128 : (group + 1) * 128] = total[g : g + 1]


def per_device(conductivity, source_field, shifts, residues, receivers):
    layers, rows, depth = conductivity.shape
    half = rows // 2
    gates, poles = residues.shape
    count = receivers.shape[0]
    groups = count // 128
    size = lax.axis_size("space")
    f32 = jnp.float32
    message = jax.ShapeDtypeStruct((10 * half + 4 * TILE, depth), f32)
    hbm = pl.BlockSpec(memory_space=pltpu.HBM)

    first, second, own_cond, own_field, own_ends = pl.pallas_call(
        send_kernel,
        out_shape=[
            message,
            message,
            jax.ShapeDtypeStruct((layers, half + TILE, depth), f32),
            jax.ShapeDtypeStruct((layers, 3, half + TILE, depth), f32),
            jax.ShapeDtypeStruct((TILE, 128), f32),
        ],
        in_specs=[hbm, hbm],
        out_specs=[VMEM] * 5,
        scratch_shapes=[
            pltpu.VMEM((layers, rows, depth), f32),
            pltpu.VMEM((3, layers, rows, depth), f32),
            pltpu.SemaphoreType.DMA((4,)),
        ],
        compiler_params=PARAMS,
        name="send",
    )(conductivity, source_field)
    far_pairs = [(i, i + 1) for i in range(1, size - 1, 2)]
    far_pairs = far_pairs + [(j, i) for i, j in far_pairs]
    second = lax.ppermute(second, "space", far_pairs)
    first = lax.ppermute(first, "space", [(i, i ^ 1) for i in range(size)])

    listed, params = pl.pallas_call(
        functools.partial(list_kernel, layers=layers, rows=rows, depth=depth),
        out_shape=[
            jax.ShapeDtypeStruct((count + 1,), jnp.int32),
            jax.ShapeDtypeStruct((TILE + 16, 128), f32),
        ],
        in_specs=[SMEM, VMEM, VMEM],
        out_specs=[SMEM, VMEM],
        scratch_shapes=[pltpu.VMEM((TILE, 128), f32)],
        compiler_params=PARAMS,
        name="owned",
    )(receivers, shifts.reshape(1, poles), residues.T)

    def field(slots):
        return pltpu.VMEM((slots, 3, half + TILE, depth), f32)

    basis, sel = pl.pallas_call(
        basis_kernel,
        out_shape=[
            jax.ShapeDtypeStruct((layers * SLOTS * half, depth), f32),
            jax.ShapeDtypeStruct((groups, SLOTS + TILE, 128), f32),
        ],
        in_specs=[VMEM] * 5 + [hbm],
        out_specs=[VMEM, VMEM],
        scratch_shapes=[
            pltpu.VMEM((layers + 4, half + TILE, depth), f32),
            pltpu.VMEM((2, half + TILE, depth), f32),
            pltpu.VMEM((2, half + TILE, depth), f32),
            *[field(layers + 4) for _ in range(6)],
            pltpu.SMEM((count + 1,), jnp.int32),
            pltpu.SemaphoreType.DMA(()),
        ],
        compiler_params=PARAMS,
        name="basis",
    )(own_cond, own_field, own_ends, first, second, listed)
    basis = basis.reshape(layers, SLOTS, half, depth)

    is_end = lax.broadcasted_iota(jnp.int32, sel.shape, 1) >= SLOTS
    stride = 2
    while stride < size:
        other = lax.ppermute(sel, "space", [(i, i ^ stride) for i in range(size)])
        sel = jnp.where(is_end, jnp.maximum(sel, other), sel + other)
        stride *= 2
    ends = sel
    sel = sel[:, :SLOTS]
    other = lax.ppermute(sel, "space", [(i, i ^ 1) for i in range(size)])

    early = layers - 1
    gated_shape = jax.ShapeDtypeStruct((gates, 3, layers, half, depth), f32)
    gated, w = pl.pallas_call(
        functools.partial(gate_kernel, poles=poles),
        grid=(early,),
        out_shape=[gated_shape, jax.ShapeDtypeStruct((WORDS, 16, 128), f32)],
        in_specs=[
            pl.BlockSpec(ends.shape, lambda i: (0, 0, 0)),
            pl.BlockSpec(params.shape, lambda i: (0, 0)),
            pl.BlockSpec((1, SLOTS, half, depth), lambda i: (i, 0, 0, 0)),
        ],
        out_specs=[
            pl.BlockSpec((gates, 3, 1, half, depth), lambda i: (0, 0, i, 0, 0)),
            pl.BlockSpec((WORDS, 16, 128), lambda i: (0, 0, 0)),
        ],
        compiler_params=PARAMS,
        cost_estimate=pl.CostEstimate(flops=2**24, bytes_accessed=2**23, transcendentals=0),
        name="gates",
    )(ends, params, basis)

    sel, w = lax.optimization_barrier((sel + other, w))
    other = lax.ppermute(sel, "pole", [(0, 1), (1, 0)])
    gated = pl.pallas_call(
        rest_kernel,
        grid=(layers - early,),
        out_shape=gated_shape,
        in_specs=[
            pl.BlockSpec(w.shape, lambda i: (0, 0, 0)),
            pl.BlockSpec((1, SLOTS, half, depth), lambda i: (i + early, 0, 0, 0)),
            hbm,
        ],
        out_specs=pl.BlockSpec((gates, 3, 1, half, depth), lambda i: (0, 0, i + early, 0, 0)),
        input_output_aliases={2: 0},
        compiler_params=PARAMS,
        cost_estimate=pl.CostEstimate(flops=2**22, bytes_accessed=2**21, transcendentals=0),
        name="rest",
    )(w, basis, gated)
    sel = sel + other

    traces = pl.pallas_call(
        trace_kernel,
        out_shape=jax.ShapeDtypeStruct((gates, 3, count), f32),
        in_specs=[VMEM, VMEM],
        out_specs=VMEM,
        compiler_params=PARAMS,
        name="traces",
    )(w, sel)
    return gated, traces


def solution(mesh):
    placed = (
        P(("survey", "space"), None, None),
        P(None, ("survey", "space"), None, None),
        P(),
        P(),
        P("survey"),
    )
    return jax.shard_map(
        per_device,
        mesh=mesh,
        in_specs=placed,
        out_specs=(P(None, None, ("survey", "space"), "pole", None), P(None, None, "survey")),
        check_vma=False,
    )
```

profile of v0, /device:TPU:1, one launch (start us, length us, event | category | flops | bytes accessed | tf_op | source)
XLA Modules:
  0.0 35.2 jit_solution(8599760864066583017)
XLA Ops:
  0.6 0.0 copy-start
  0.6 1.0 %copy-done = f32[3,4,64,128]{3,2,1,0:T(8,128)S(1)} copy-done((f32[3,4,64,128]{3,2,1,0:T(8,128)S(1)}, f32[3,4,64,128]{3,2,1,0:T(8,128)}, u32[]{:S(2)}) %copy-start) | copy-done | bytes 393240
  1.6 0.0 copy-start.1
  1.6 0.9 %copy-done.1 = f32[4,64,128]{2,1,0:T(8,128)S(1)} copy-done((f32[4,64,128]{2,1,0:T(8,128)S(1)}, f32[4,64,128]{2,1,0:T(8,128)}, u32[]{:S(2)}) %copy-start.1) | copy-done | bytes 131096
  2.5 0.8 %send.1 = (f32[352,128]{1,0:T(8,128)S(1)}, f32[352,128]{1,0:T(8,128)S(1)}, f32[4,40,128]{2,1,0:T(8,128)S(1)}, f32[4,3,40,128]{3,2,1,0:T(8,128)S(1)}, f32[8,128]{1,0:T(8,128)S(1)}) custom-call(f32[4,64,128]{2,1,0:T(8,128)S(1)} %copy-done.1, f32[3,4,64,128]{3,2,1,0:T(8,128)S(1)} %copy-done), custom_call_target="tpu_custom_call" | custom-call | tf_op jit(solution)/shard_map/send/pallas_call | solution.py:454
  3.4 2.1 %collective-permute-start = (f32[352,128]{1,0:T(8,128)S(1)}, f32[352,128]{1,0:T(8,128)S(1)}, u32[]{:S(2)}, u32[]{:S(2)}) collective-permute-start(f32[352,128]{1,0:T(8,128)S(1)} %get-tuple-element.18), channel_id=1, source_target_pairs={{0,1},{1,0},{2,3},{3,2},{4,5},{5,4},{6,7},{7,6},{8,9},{9,8},{10,11... | collective-permute-start | bytes 540680 | tf_op jit(solution)/shard_map/ppermute | solution.py:476
  5.5 0.7 %collective-permute-start.1 = (f32[352,128]{1,0:T(8,128)S(1)}, f32[352,128]{1,0:T(8,128)S(1)}, u32[]{:S(2)}, u32[]{:S(2)}) collective-permute-start(f32[352,128]{1,0:T(8,128)S(1)} %get-tuple-element.19), channel_id=1, source_target_pairs={{1,2},{3,4},{5,6},{2,1},{4,3},{6,5},{9,10},{11,12},{13,14},{10,9},... | collective-permute-start | bytes 540680 | tf_op jit(solution)/shard_map/ppermute | solution.py:475
  6.2 0.0 copy-start.2
  6.2 0.7 %copy-done.2 = f32[12,8]{0,1:T(8,128)S(1)} copy-done((f32[12,8]{0,1:T(8,128)S(1)}, f32[12,8]{0,1:T(8,128)}, u32[]{:S(2)}) %copy-start.2) | copy-done | bytes 408
  6.9 0.0 copy-start.3
  6.9 0.7 %copy-done.3 = s32[256]{0:T(256)S(1)} copy-done((s32[256]{0:T(256)S(1)}, s32[256]{0:T(256)}, u32[]{:S(2)}) %copy-start.3) | copy-done | bytes 1048
  7.5 0.0 copy-start.4
  7.5 0.7 %copy-done.4 = f32[8]{0:T(128)S(1)} copy-done((f32[8]{0:T(128)S(1)}, f32[8]{0:T(128)}, u32[]{:S(2)}) %copy-start.4) | copy-done | bytes 56
  8.2 4.1 %owned.1 = (s32[257]{0:T(512)S(1)}, f32[24,128]{1,0:T(8,128)S(1)}) custom-call(s32[256]{0:T(256)S(1)} %copy-done.3, f32[1,8]{1,0:T(1,128)S(1)} %bitcast.6, f32[8,12]{1,0:T(8,128)S(1)} %bitcast.5), custom_call_target="tpu_custom_call" | custom-call | tf_op jit(solution)/shard_map/owned/pallas_call | solution.py:478
  12.3 0.0 collective-permute-done.first_ref
  12.3 0.0 collective-permute-done.1.second_ref
  12.4 4.3 %basis.1 = (f32[4096,128]{1,0:T(8,128)S(1)}, f32[2,40,128]{2,1,0:T(8,128)S(1)}) custom-call(f32[4,40,128]{2,1,0:T(8,128)S(1)} %get-tuple-element.15.cond_ref, f32[4,3,40,128]{3,2,1,0:T(8,128)S(1)} %get-tuple-element.16.field_ref, f32[8,128]{1,0:T(8,128)S(1)} %get-tuple-element.17.ends_ref, f32[352,128]{1,0:T(8,128)S(1)} %collective-permute-done.first_ref, ...), custom_call_target="tpu_custom_call" | custom-call | tf_op jit(solution)/shard_map/basis/pallas_call | solution.py:494
  16.6 2.3 %collective-permute-start.2 = (f32[2,40,128]{2,1,0:T(8,128)S(1)}, f32[2,40,128]{2,1,0:T(8,128)S(1)}, u32[]{:S(2)}, u32[]{:S(2)}) collective-permute-start(f32[2,40,128]{2,1,0:T(8,128)S(1)} %get-tuple-element.21), channel_id=1, source_target_pairs={{0,2},{1,3},{2,0},{3,1},{4,6},{5,7},{6,4},{7,5},{8,10},{9,11},{10,... | collective-permute-start | bytes 122888 | tf_op jit(solution)/shard_map/ppermute | solution.py:518
  18.9 1.4 %collective-permute-done.2 = f32[2,40,128]{2,1,0:T(8,128)S(1)} collective-permute-done((f32[2,40,128]{2,1,0:T(8,128)S(1)}, f32[2,40,128]{2,1,0:T(8,128)S(1)}, u32[]{:S(2)}, u32[]{:S(2)}) %collective-permute-start.2) | collective-permute-done | bytes 40992 | tf_op jit(solution)/shard_map/ppermute | solution.py:518
  20.3 0.1 add_select_fusion.1
  20.4 1.9 %collective-permute-start.3 = (f32[2,40,128]{2,1,0:T(8,128)S(1)}, f32[2,40,128]{2,1,0:T(8,128)S(1)}, u32[]{:S(2)}, u32[]{:S(2)}) collective-permute-start(f32[2,40,128]{2,1,0:T(8,128)S(1)} %add_select_fusion.1), channel_id=1, source_target_pairs={{0,4},{1,5},{2,6},{3,7},{4,0},{5,1},{6,2},{7,3},{8,12},{9,13},{10,... | collective-permute-start | bytes 122888 | tf_op jit(solution)/shard_map/ppermute | solution.py:518
  22.3 1.8 %collective-permute-done.3 = f32[2,40,128]{2,1,0:T(8,128)S(1)} collective-permute-done((f32[2,40,128]{2,1,0:T(8,128)S(1)}, f32[2,40,128]{2,1,0:T(8,128)S(1)}, u32[]{:S(2)}, u32[]{:S(2)}) %collective-permute-start.3) | collective-permute-done | bytes 40992 | tf_op jit(solution)/shard_map/ppermute | solution.py:518
  24.1 0.1 add_select_fusion.ends_ref
  24.2 2.5 %collective-permute-start.4 = (f32[2,32,128]{2,1,0:T(8,128)S(1)}, f32[2,32,128]{2,1,0:T(8,128)S(1)}, u32[]{:S(2)}, u32[]{:S(2)}) collective-permute-start(f32[2,32,128]{2,1,0:T(8,128)S(1)} %slice.4), channel_id=1, source_target_pairs={{0,1},{1,0},{2,3},{3,2},{4,5},{5,4},{6,7},{7,6},{8,9},{9,8},{10,11... | collective-permute-start | bytes 98312 | tf_op jit(solution)/shard_map/ppermute | solution.py:523
  26.7 2.7 %gates.1 = (f32[12,3,4,32,128]{4,3,2,1,0:T(8,128)}, f32[10,16,128]{2,1,0:T(8,128)S(1)}) custom-call(f32[2,40,128]{2,1,0:T(8,128)S(1)} %add_select_fusion.ends_ref, f32[24,128]{1,0:T(8,128)S(1)} %get-tuple-element.22.par_ref, f32[4,32,32,128]{3,2,1,0:T(8,128)S(1)} %bitcast.3), custom_call_target="tpu_custom_call" | custom-call | flops 16777216 | bytes 8388608 | tf_op jit(solution)/shard_map/gates/pallas_call | solution.py:527
  29.4 0.0 collective-permute-done.4
  29.4 3.9 %collective-permute-start.5 = (f32[2,32,128]{2,1,0:T(8,128)S(1)}, f32[2,32,128]{2,1,0:T(8,128)S(1)}, u32[]{:S(2)}, u32[]{:S(2)}) collective-permute-start(f32[2,32,128]{2,1,0:T(8,128)S(1)} %slice_add_fusion), channel_id=1, source_target_pairs={{0,8},{8,0},{1,9},{9,1},{2,10},{10,2},{3,11},{11,3},{4,12},{12,4},... | collective-permute-start | bytes 98312 | tf_op jit(solution)/shard_map/ppermute | solution.py:546
  33.3 1.2 %rest.1 = f32[12,3,4,32,128]{4,3,2,1,0:T(8,128)} custom-call(f32[10,16,128]{2,1,0:T(8,128)S(1)} %get-tuple-element.25.w_ref, f32[4,32,32,128]{3,2,1,0:T(8,128)S(1)} %bitcast.4, f32[12,3,4,32,128]{4,3,2,1,0:T(8,128)} %get-tuple-element.26.before_ref), custom_call_target="tpu_custom_call", output_to_operand_aliasing={{}: (2, {})} | custom-call | flops 4194304 | bytes 2097152 | tf_op jit(solution)/shard_map/rest/pallas_call | solution.py:547
  34.5 0.0 collective-permute-done.5
  34.5 0.7 %traces.1 = f32[12,3,256]{2,1,0:T(4,128)} custom-call(f32[10,16,128]{2,1,0:T(8,128)S(1)} %get-tuple-element.25.w_ref, f32[2,32,128]{2,1,0:T(8,128)S(1)} %add.15.sel_ref), custom_call_target="tpu_custom_call" | custom-call | tf_op jit(solution)/shard_map/traces/pallas_call | solution.py:564
  (4 shorter events, 0.0 us)
Async XLA Ops:
  0.6 1.0 %copy-start = (f32[3,4,64,128]{3,2,1,0:T(8,128)S(1)}, f32[3,4,64,128]{3,2,1,0:T(8,128)}, u32[]{:S(2)}) copy-start(f32[3,4,64,128]{3,2,1,0:T(8,128)} %src_hbm.1) | copy-start | bytes 1179652
  1.6 0.9 %copy-start.1 = (f32[4,64,128]{2,1,0:T(8,128)S(1)}, f32[4,64,128]{2,1,0:T(8,128)}, u32[]{:S(2)}) copy-start(f32[4,64,128]{2,1,0:T(8,128)} %cond_hbm.1) | copy-start | bytes 393220
  3.4 9.0 %collective-permute-start = (f32[352,128]{1,0:T(8,128)S(1)}, f32[352,128]{1,0:T(8,128)S(1)}, u32[]{:S(2)}, u32[]{:S(2)}) collective-permute-start(f32[352,128]{1,0:T(8,128)S(1)} %get-tuple-element.18), channel_id=1, source_target_pairs={{0,1},{1,0},{2,3},{3,2},{4,5},{5,4},{6,7},{7,6},{8,9},{9,8},{10,11... | collective-permute-start | bytes 540680 | tf_op jit(solution)/shard_map/ppermute | solution.py:476
  5.5 6.8 %collective-permute-start.1 = (f32[352,128]{1,0:T(8,128)S(1)}, f32[352,128]{1,0:T(8,128)S(1)}, u32[]{:S(2)}, u32[]{:S(2)}) collective-permute-start(f32[352,128]{1,0:T(8,128)S(1)} %get-tuple-element.19), channel_id=1, source_target_pairs={{1,2},{3,4},{5,6},{2,1},{4,3},{6,5},{9,10},{11,12},{13,14},{10,9},... | collective-permute-start | bytes 540680 | tf_op jit(solution)/shard_map/ppermute | solution.py:475
  6.2 0.7 %copy-start.2 = (f32[12,8]{0,1:T(8,128)S(1)}, f32[12,8]{0,1:T(8,128)}, u32[]{:S(2)}) copy-start(f32[12,8]{0,1:T(8,128)} %param.8) | copy-start | bytes 1156
  6.9 0.7 %copy-start.3 = (s32[256]{0:T(256)S(1)}, s32[256]{0:T(256)}, u32[]{:S(2)}) copy-start(s32[256]{0:T(256)} %rec_ref.1) | copy-start | bytes 3076
  7.5 0.7 %copy-start.4 = (f32[8]{0:T(128)S(1)}, f32[8]{0:T(128)}, u32[]{:S(2)}) copy-start(f32[8]{0:T(128)} %param.7) | copy-start | bytes 100
  16.6 3.6 %collective-permute-start.2 = (f32[2,40,128]{2,1,0:T(8,128)S(1)}, f32[2,40,128]{2,1,0:T(8,128)S(1)}, u32[]{:S(2)}, u32[]{:S(2)}) collective-permute-start(f32[2,40,128]{2,1,0:T(8,128)S(1)} %get-tuple-element.21), channel_id=1, source_target_pairs={{0,2},{1,3},{2,0},{3,1},{4,6},{5,7},{6,4},{7,5},{8,10},{9,11},{10,... | collective-permute-start | bytes 122888 | tf_op jit(solution)/shard_map/ppermute | solution.py:518
  20.4 3.8 %collective-permute-start.3 = (f32[2,40,128]{2,1,0:T(8,128)S(1)}, f32[2,40,128]{2,1,0:T(8,128)S(1)}, u32[]{:S(2)}, u32[]{:S(2)}) collective-permute-start(f32[2,40,128]{2,1,0:T(8,128)S(1)} %add_select_fusion.1), channel_id=1, source_target_pairs={{0,4},{1,5},{2,6},{3,7},{4,0},{5,1},{6,2},{7,3},{8,12},{9,13},{10,... | collective-permute-start | bytes 122888 | tf_op jit(solution)/shard_map/ppermute | solution.py:518
  24.2 5.2 %collective-permute-start.4 = (f32[2,32,128]{2,1,0:T(8,128)S(1)}, f32[2,32,128]{2,1,0:T(8,128)S(1)}, u32[]{:S(2)}, u32[]{:S(2)}) collective-permute-start(f32[2,32,128]{2,1,0:T(8,128)S(1)} %slice.4), channel_id=1, source_target_pairs={{0,1},{1,0},{2,3},{3,2},{4,5},{5,4},{6,7},{7,6},{8,9},{9,8},{10,11... | collective-permute-start | bytes 98312 | tf_op jit(solution)/shard_map/ppermute | solution.py:523
  29.4 5.1 %collective-permute-start.5 = (f32[2,32,128]{2,1,0:T(8,128)S(1)}, f32[2,32,128]{2,1,0:T(8,128)S(1)}, u32[]{:S(2)}, u32[]{:S(2)}) collective-permute-start(f32[2,32,128]{2,1,0:T(8,128)S(1)} %slice_add_fusion), channel_id=1, source_target_pairs={{0,8},{8,0},{1,9},{9,1},{2,10},{10,2},{3,11},{11,3},{4,12},{12,4},... | collective-permute-start | bytes 98312 | tf_op jit(solution)/shard_map/ppermute | solution.py:546
where the time goes:
time: 35.3 us; the launch traced here: 35.2 us
  Pallas kernels  13.8 us (39%)
  starting transfers between devices  13.4 us (38%)
  local copies, waits for them, and re-layouts  3.91 us (11%)
  waiting for transfers between devices  3.2 us (9%)
  between operations  0.71 us (2%)
    pallas_call x1, Pallas kernels, per_device(): pl.pallas_call(basis_kernel, out_shape=[jax.ShapeDtypeStruct((layers * SL...  4.27 us
    ppermute x2, starting transfers between devices, per_device(): other = lax.ppermute(sel, 'space', [(i, i ^ stride) for i in range(size)])  4.2 us
    pallas_call x1, Pallas kernels, per_device(): pl.pallas_call(functools.partial(list_kernel, layers=layers, rows=rows, d...  4.13 us
    unnamed x10, local copies, waits for them, and re-layouts  3.91 us
    ppermute x1, starting transfers between devices, per_device(): other = lax.ppermute(sel, 'pole', [(0, 1), (1, 0)])  3.88 us
    ppermute x2, waiting for transfers between devices, per_device(): other = lax.ppermute(sel, 'space', [(i, i ^ stride) for i in range(size)])  3.19 us
    pallas_call x1, Pallas kernels, per_device(): pl.pallas_call(functools.partial(gate_kernel, poles=poles), grid=(early,)...  2.66 us
    ppermute x1, starting transfers between devices, per_device(): other = lax.ppermute(sel, 'space', [(i, i ^ 1) for i in range(size)])  2.52 us
  transfers between devices with their start and end apart: 6, of which 2 were waited for; matrix products, arithmetic and copies ran while one was open for 0% of the time, Pallas kernels for 23%

commit v1 on v0

--- a/solution.py
+++ b/solution.py
@@ -9,7 +9,12 @@
 
 MID = 4.65
 WORDS = 10
-SLOTS = 32
+POINTWISE = (0, 2, 5, 9)
+FIELDS = (1, 3, 4, 6, 7, 8)
+SIGMA = 3 * (1 + len(FIELDS))
+ENDS = SIGMA + 1
+SLOTS = ENDS + 2
+PICKS = 4
 TILE = 8
 VMEM = pl.BlockSpec(memory_space=pltpu.VMEM)
 SMEM = pl.BlockSpec(memory_space=pltpu.SMEM)
@@ -38,6 +43,16 @@
 
 def lane_prev(v, first):
     return jnp.where(lanes_of(v) == 0, first, pltpu.roll(v, 1, 1))
+
+
+def split(value, size):
+    if size & (size - 1):
+        return lax.div(value, size), lax.rem(value, size)
+    return value >> (size.bit_length() - 1), value & (size - 1)
+
+
+def bits_of(size):
+    return (size - 1).bit_length()
 
 
 def part_keep(core):
@@ -155,13 +170,16 @@
     half = rows // 2
     total = rec_ref.shape[0]
 
+    bits = bits_of(total)
+
     def step(at, count):
-        cell = rec_ref[at]
-        x = lax.div(cell, rows * depth) - base
-        y = lax.rem(lax.div(cell, depth), rows) - core * half
+        line, z = split(rec_ref[at], depth)
+        x, y = split(line, rows)
+        x, y = x - base, y - core * half
         owned = (x >= 0) & (x < layers) & (y >= 0) & (y < half)
         start = x * (SLOTS * half) + y
-        list_ref[count] = (start * depth + lax.rem(cell, depth)) * total + at
+        turn = (at - z) & 127
+        list_ref[count] = (((start << 7) | turn) << bits) | at
         return count + owned.astype(jnp.int32)
 
     list_ref[total] = lax.fori_loop(0, total, step, jnp.int32(0), unroll=8)
@@ -297,12 +315,10 @@
     inner = list(range(2, layers + 2))
     for slot in inner:
         for c in range(3):
-            for word, ref in enumerate((t00, t10, t11, t20, t21, t22)):
+            for word, ref in enumerate((t00, t10, t20, t21)):
                 store(word, slot, c, ref[slot, c, :half, :])
-            store(9, slot, c, sig[slot, :half, :] * t22[slot, c, :half, :])
-        for spare in range(WORDS * 3, SLOTS):
-            base = ((slot - 2) * SLOTS + spare) * half
-            bas_ref[base : base + half, :] = jnp.zeros((half, depth), jnp.float32)
+        base = ((slot - 2) * SLOTS + SIGMA) * half
+        bas_ref[base : base + half, :] = sig[slot, :half, :]
 
     def put_3(word, before):
         def put(slot, out):
@@ -314,42 +330,43 @@
 
         return put
 
-    curl_curl(sums(t20), reader(t20), inner, put_3(6, None), half)
-    curl_curl(sums(t21), reader(t21), inner, put_3(7, t20), half)
-    curl_curl(sums(t22), reader(t22), inner, put_3(8, t21), half)
+    curl_curl(sums(t20), reader(t20), inner, put_3(4, None), half)
+    curl_curl(sums(t21), reader(t21), inner, put_3(5, t20), half)
+    curl_curl(sums(t22), reader(t22), inner, put_3(6, t21), half)
 
     groups = sel_ref.shape[0]
+    lane = lax.broadcasted_iota(jnp.int32, (SLOTS, depth), 1)
+    total = list_ref.shape[0] - 1
+    bits = bits_of(total)
+    list_copy.wait()
+    owned = list_ref[total]
+
+    def pick(turn, found):
+        for step in range(PICKS):
+            at = turn * PICKS + step
+            code = jnp.where(at < owned, list_ref[jnp.minimum(at, total - 1)], 0)
+            which = jnp.where(at < owned, code & ((1 << bits) - 1), -1)
+            block = bas_ref[pl.ds(code >> (7 + bits), SLOTS, stride=half), :]
+            block = pltpu.roll(block, (code >> bits) & 127, 1)
+            found = [
+                jnp.where(lane == which - 128 * group, block, value)
+                for group, value in enumerate(found)
+            ]
+        return found
+
+    zero = jnp.zeros((SLOTS, depth), jnp.float32)
+    found = lax.fori_loop(0, (owned + PICKS - 1) // PICKS, pick, [zero] * groups)
     for group in range(groups):
-        sel_ref[group, :SLOTS, :] = jnp.zeros((SLOTS, depth), jnp.float32)
+        sel_ref[group] = found[group]
+
     tile = first_ref[10 * half + 3 * TILE : 10 * half + 4 * TILE, :]
-    row = lax.broadcasted_iota(jnp.int32, (TILE, 128), 0)
-    ends = jnp.maximum(ends_ref[...], jnp.where(row == 0, tile[6:7], tile[7:8]))
     for group in range(groups):
-        sel_ref[group, SLOTS:, :] = ends
-
-    lane = lax.broadcasted_iota(jnp.int32, (SLOTS, depth), 1)
-
-    total = list_ref.shape[0] - 1
-    list_copy.wait()
-
-    def pick(at, carry):
-        code = list_ref[at]
-        which = lax.rem(code, total)
-        cell = lax.div(code, total)
-        z = lax.rem(cell, depth)
-        block = bas_ref[pl.ds(lax.div(cell, depth), SLOTS, stride=half), :]
-        target = lax.rem(which, 128)
-        group = lax.div(which, 128)
-        block = pltpu.roll(block, lax.rem(target - z + 128, 128), 1)
-        sel_ref[group, :SLOTS, :] = jnp.where(lane == target, block, sel_ref[group, :SLOTS, :])
-        return carry
-
-    lax.fori_loop(0, list_ref[total], pick, 0)
+        sel_ref[group, ENDS:, :] = jnp.maximum(ends_ref[:2, :], tile[TILE - 2 :])
 
 
 def weights(ends_ref, par_ref, out_ref, gates, poles):
-    upper = jnp.max(ends_ref[0, SLOTS : SLOTS + 1, :], axis=1, keepdims=True)
-    lower = -jnp.max(ends_ref[0, SLOTS + 1 : SLOTS + 2, :], axis=1, keepdims=True)
+    upper = jnp.max(ends_ref[0, ENDS : ENDS + 1, :], axis=1, keepdims=True)
+    lower = -jnp.max(ends_ref[0, ENDS + 1 : ENDS + 2, :], axis=1, keepdims=True)
     shift = jnp.where(lax.broadcasted_iota(jnp.int32, (1, 128), 1) < poles, par_ref[:1, :], 1.0)
     low_end = shift * lower
     high_end = 16.0 + shift * upper
@@ -400,16 +417,27 @@
             word += 1
 
 
-def combine(w_ref, bas_ref, out_ref, gates):
+def power_sum(weight, moved):
+    total = weight(POINTWISE[3])
+    for word in POINTWISE[2::-1]:
+        total = total * moved + weight(word)
+    return total
+
+
+def combine(w_ref, bas_ref, out_ref, gates, layer):
     half = bas_ref.shape[2]
-    for c in range(3):
-        for top in range(0, half, TILE):
-            terms = [bas_ref[0, word * 3 + c, top : top + TILE, :] for word in range(WORDS)]
-            for g in range(gates):
-                total = w_ref[0, g : g + 1, :] * terms[0]
-                for word in range(1, WORDS):
-                    total = total + w_ref[word, g : g + 1, :] * terms[word]
-                out_ref[g, c, 0, top : top + TILE, :] = total
+    for top in range(0, half, TILE):
+        part = slice(top, top + TILE)
+        moved = bas_ref[layer, SIGMA, part, :]
+        fields = [bas_ref[layer, at, part, :] for at in range(SIGMA)]
+        for g in range(gates):
+            weight = lambda word: w_ref[word, g : g + 1, :]
+            scale = power_sum(weight, moved)
+            for c in range(3):
+                total = scale * fields[c]
+                for at, word in enumerate(FIELDS, 1):
+                    total = total + weight(word) * fields[at * 3 + c]
+                out_ref[g, c, 0, part, :] = total
 
 
 def gate_kernel(ends_ref, par_ref, bas_ref, out_ref, w_ref, *, poles):
@@ -419,23 +447,23 @@
     def _():
         weights(ends_ref, par_ref, w_ref, gates, poles)
 
-    combine(w_ref, bas_ref, out_ref, gates)
-
-
-def rest_kernel(w_ref, bas_ref, before_ref, out_ref):
+    combine(w_ref, bas_ref, out_ref, gates, pl.program_id(0))
+
+
+def rest_kernel(w_ref, bas_ref, before_ref, out_ref, *, early):
     del before_ref
-    combine(w_ref, bas_ref, out_ref, out_ref.shape[0])
+    combine(w_ref, bas_ref, out_ref, out_ref.shape[0], pl.program_id(0) + early)
 
 
 def trace_kernel(w_ref, sel_ref, out_ref):
     gates = out_ref.shape[0]
+    weight = lambda word: w_ref[word, :gates, :]
     for group in range(sel_ref.shape[0]):
+        scale = power_sum(weight, sel_ref[group, SIGMA : SIGMA + 1, :])
         for c in range(3):
-            total = None
-            for word in range(WORDS):
-                at = word * 3 + c
-                term = w_ref[word, :gates, :] * sel_ref[group, at : at + 1, :]
-                total = term if total is None else total + term
+            total = scale * sel_ref[group, c : c + 1, :]
+            for at, word in enumerate(FIELDS, 1):
+                total = total + weight(word) * sel_ref[group, at * 3 + c : at * 3 + c + 1, :]
             for g in range(gates):
                 out_ref[g, c : c + 1, group * 128 : (group + 1) * 128] = total[g : g + 1]
 
@@ -467,7 +495,7 @@
             pltpu.VMEM((3, layers, rows, depth), f32),
             pltpu.SemaphoreType.DMA((4,)),
         ],
-        compiler_params=PARAMS,
+        compiler_params=pltpu.CompilerParams(vmem_limit_bytes=53 * 1024 * 1024),
         name="send",
     )(conductivity, source_field)
     far_pairs = [(i, i + 1) for i in range(1, size - 1, 2)]
@@ -495,7 +523,7 @@
         basis_kernel,
         out_shape=[
             jax.ShapeDtypeStruct((layers * SLOTS * half, depth), f32),
-            jax.ShapeDtypeStruct((groups, SLOTS + TILE, 128), f32),
+            jax.ShapeDtypeStruct((groups, SLOTS, 128), f32),
         ],
         in_specs=[VMEM] * 5 + [hbm],
         out_specs=[VMEM, VMEM],
@@ -512,14 +540,13 @@
     )(own_cond, own_field, own_ends, first, second, listed)
     basis = basis.reshape(layers, SLOTS, half, depth)
 
-    is_end = lax.broadcasted_iota(jnp.int32, sel.shape, 1) >= SLOTS
+    is_end = lax.broadcasted_iota(jnp.int32, sel.shape, 1) >= ENDS
     stride = 2
     while stride < size:
         other = lax.ppermute(sel, "space", [(i, i ^ stride) for i in range(size)])
         sel = jnp.where(is_end, jnp.maximum(sel, other), sel + other)
         stride *= 2
     ends = sel
-    sel = sel[:, :SLOTS]
     other = lax.ppermute(sel, "space", [(i, i ^ 1) for i in range(size)])
 
     early = layers - 1
@@ -529,9 +556,9 @@
         grid=(early,),
         out_shape=[gated_shape, jax.ShapeDtypeStruct((WORDS, 16, 128), f32)],
         in_specs=[
-            pl.BlockSpec(ends.shape, lambda i: (0, 0, 0)),
-            pl.BlockSpec(params.shape, lambda i: (0, 0)),
-            pl.BlockSpec((1, SLOTS, half, depth), lambda i: (i, 0, 0, 0)),
+            VMEM,
+            VMEM,
+            VMEM,
         ],
         out_specs=[
             pl.BlockSpec((gates, 3, 1, half, depth), lambda i: (0, 0, i, 0, 0)),
@@ -545,12 +572,12 @@
     sel, w = lax.optimization_barrier((sel + other, w))
     other = lax.ppermute(sel, "pole", [(0, 1), (1, 0)])
     gated = pl.pallas_call(
-        rest_kernel,
+        functools.partial(rest_kernel, early=early),
         grid=(layers - early,),
         out_shape=gated_shape,
         in_specs=[
-            pl.BlockSpec(w.shape, lambda i: (0, 0, 0)),
-            pl.BlockSpec((1, SLOTS, half, depth), lambda i: (i + early, 0, 0, 0)),
+            VMEM,
+            VMEM,
             hbm,
         ],
         out_specs=pl.BlockSpec((gates, 3, 1, half, depth), lambda i: (0, 0, i + early, 0, 0)),

time: 35.3 us -> 32.8 us (0.929)
  Pallas kernels: 13.8 us -> 12.1 us
  local copies, waits for them, and re-layouts: 3.91 us -> 2.91 us
  starting transfers between devices: 13.4 us -> 14.3 us
  waiting for transfers between devices: 3.2 us -> 2.44 us
    ppermute x2, starting transfers between devices: 4.2 us -> 5.56 us  [per_device(): other = lax.ppermute(sel, 'space', [(i, i ^ stride) for i in range(size)])]
    pallas_call x1, Pallas kernels: 4.27 us -> 3.12 us  [per_device(): pl.pallas_call(basis_kernel, out_shape=[jax.ShapeDtypeStruct((layers * SL...]
    unnamed x10 -> x8, local copies, waits for them, and re-layouts: 3.91 us -> 2.91 us
    pallas_call x1, Pallas kernels: 4.13 us -> 3.31 us  [per_device(): pl.pallas_call(functools.partial(list_kernel, layers=layers, rows=rows, d...]
    ppermute x2, waiting for transfers between devices: 3.19 us -> 2.43 us  [per_device(): other = lax.ppermute(sel, 'space', [(i, i ^ stride) for i in range(size)])]
    pallas_call x1, Pallas kernels: 0.83 us -> 1.34 us  [per_device(): pl.pallas_call(send_kernel, out_shape=[message, message, jax.ShapeDtypeSt...]
  transfers between devices with their start and end apart: 6 -> 6, of which waited for: 2 -> 2; matrix products, arithmetic and copies ran while one was open for 0% -> 0% of each run, Pallas kernels for 23% -> 21%
where the time goes in v1:
time: 32.8 us; the launch traced here: 32.6 us
  starting transfers between devices  14.3 us (44%)
  Pallas kernels  12.1 us (37%)
  local copies, waits for them, and re-layouts  2.91 us (9%)
  waiting for transfers between devices  2.44 us (7%)
  between operations  0.71 us (2%)
    ppermute x2, starting transfers between devices, per_device(): other = lax.ppermute(sel, 'space', [(i, i ^ stride) for i in range(size)])  5.56 us
    ppermute x1, starting transfers between devices, per_device(): other = lax.ppermute(sel, 'pole', [(0, 1), (1, 0)])  3.64 us
    pallas_call x1, Pallas kernels, per_device(): pl.pallas_call(functools.partial(list_kernel, layers=layers, rows=rows, d...  3.31 us
    pallas_call x1, Pallas kernels, per_device(): pl.pallas_call(basis_kernel, out_shape=[jax.ShapeDtypeStruct((layers * SL...  3.12 us
    unnamed x8, local copies, waits for them, and re-layouts  2.91 us
    pallas_call x1, Pallas kernels, per_device(): pl.pallas_call(functools.partial(gate_kernel, poles=poles), grid=(early,)...  2.49 us
    ppermute x2, waiting for transfers between devices, per_device(): other = lax.ppermute(sel, 'space', [(i, i ^ stride) for i in range(size)])  2.43 us
    ppermute x1, starting transfers between devices, per_device(): other = lax.ppermute(sel, 'space', [(i, i ^ 1) for i in range(size)])  2.28 us
  transfers between devices with their start and end apart: 6, of which 2 were waited for; matrix products, arithmetic and copies ran while one was open for 0% of the time, Pallas kernels for 21%

profile of v1, /device:TPU:1, one launch (start us, length us, event | category | flops | bytes accessed | tf_op | source)
XLA Modules:
  0.0 32.6 jit_solution(2286942848453369742)
XLA Ops:
  0.6 0.0 copy-start
  0.6 0.9 %copy-done = f32[4,64,128]{2,1,0:T(8,128)S(1)} copy-done((f32[4,64,128]{2,1,0:T(8,128)S(1)}, f32[4,64,128]{2,1,0:T(8,128)}, u32[]{:S(2)}) %copy-start) | copy-done | bytes 131096
  1.5 1.3 %send.1 = (f32[352,128]{1,0:T(8,128)S(1)}, f32[352,128]{1,0:T(8,128)S(1)}, f32[4,40,128]{2,1,0:T(8,128)S(1)}, f32[4,3,40,128]{3,2,1,0:T(8,128)S(1)}, f32[8,128]{1,0:T(8,128)S(1)}) custom-call(f32[4,64,128]{2,1,0:T(8,128)S(1)} %copy-done, f32[3,4,64,128]{3,2,1,0:T(8,128)} %src_hbm.1), custom_call_target="tpu_custom_call" | custom-call | tf_op jit(solution)/shard_map/send/pallas_call | solution.py:482
  2.9 2.1 %collective-permute-start = (f32[352,128]{1,0:T(8,128)S(1)}, f32[352,128]{1,0:T(8,128)S(1)}, u32[]{:S(2)}, u32[]{:S(2)}) collective-permute-start(f32[352,128]{1,0:T(8,128)S(1)} %get-tuple-element.18), channel_id=1, source_target_pairs={{0,1},{1,0},{2,3},{3,2},{4,5},{5,4},{6,7},{7,6},{8,9},{9,8},{10,11... | collective-permute-start | bytes 540680 | tf_op jit(solution)/shard_map/ppermute | solution.py:504
  5.0 0.7 %collective-permute-start.1 = (f32[352,128]{1,0:T(8,128)S(1)}, f32[352,128]{1,0:T(8,128)S(1)}, u32[]{:S(2)}, u32[]{:S(2)}) collective-permute-start(f32[352,128]{1,0:T(8,128)S(1)} %get-tuple-element.19), channel_id=1, source_target_pairs={{1,2},{3,4},{5,6},{2,1},{4,3},{6,5},{9,10},{11,12},{13,14},{10,9},... | collective-permute-start | bytes 540680 | tf_op jit(solution)/shard_map/ppermute | solution.py:503
  5.7 0.0 copy-start.1
  5.7 0.7 %copy-done.1 = f32[12,8]{0,1:T(8,128)S(1)} copy-done((f32[12,8]{0,1:T(8,128)S(1)}, f32[12,8]{0,1:T(8,128)}, u32[]{:S(2)}) %copy-start.1) | copy-done | bytes 408
  6.4 0.0 copy-start.2
  6.4 0.7 %copy-done.2 = s32[256]{0:T(256)S(1)} copy-done((s32[256]{0:T(256)S(1)}, s32[256]{0:T(256)}, u32[]{:S(2)}) %copy-start.2) | copy-done | bytes 1048
  7.1 0.0 copy-start.3
  7.1 0.7 %copy-done.3 = f32[8]{0:T(128)S(1)} copy-done((f32[8]{0:T(128)S(1)}, f32[8]{0:T(128)}, u32[]{:S(2)}) %copy-start.3) | copy-done | bytes 56
  7.7 3.3 %owned.1 = (s32[257]{0:T(512)S(1)}, f32[24,128]{1,0:T(8,128)S(1)}) custom-call(s32[256]{0:T(256)S(1)} %copy-done.2, f32[1,8]{1,0:T(1,128)S(1)} %bitcast.6, f32[8,12]{1,0:T(8,128)S(1)} %bitcast.5), custom_call_target="tpu_custom_call" | custom-call | tf_op jit(solution)/shard_map/owned/pallas_call | solution.py:506
  11.0 0.0 collective-permute-done.first_ref
  11.1 0.0 collective-permute-done.1.second_ref
  11.1 3.1 %basis.1 = (f32[3072,128]{1,0:T(8,128)S(1)}, f32[2,24,128]{2,1,0:T(8,128)S(1)}) custom-call(f32[4,40,128]{2,1,0:T(8,128)S(1)} %get-tuple-element.15.cond_ref, f32[4,3,40,128]{3,2,1,0:T(8,128)S(1)} %get-tuple-element.16.field_ref, f32[8,128]{1,0:T(8,128)S(1)} %get-tuple-element.17.ends_ref, f32[352,128]{1,0:T(8,128)S(1)} %collective-permute-done.first_ref, ...), custom_call_target="tpu_custom_call" | custom-call | tf_op jit(solution)/shard_map/basis/pallas_call | solution.py:522
  14.2 3.1 %collective-permute-start.2 = (f32[2,24,128]{2,1,0:T(8,128)S(1)}, f32[2,24,128]{2,1,0:T(8,128)S(1)}, u32[]{:S(2)}, u32[]{:S(2)}) collective-permute-start(f32[2,24,128]{2,1,0:T(8,128)S(1)} %get-tuple-element.21), channel_id=1, source_target_pairs={{0,2},{1,3},{2,0},{3,1},{4,6},{5,7},{6,4},{7,5},{8,10},{9,11},{10,... | collective-permute-start | bytes 73736 | tf_op jit(solution)/shard_map/ppermute | solution.py:546
  17.3 1.2 %collective-permute-done.2 = f32[2,24,128]{2,1,0:T(8,128)S(1)} collective-permute-done((f32[2,24,128]{2,1,0:T(8,128)S(1)}, f32[2,24,128]{2,1,0:T(8,128)S(1)}, u32[]{:S(2)}, u32[]{:S(2)}) %collective-permute-start.2) | collective-permute-done | bytes 24608 | tf_op jit(solution)/shard_map/ppermute | solution.py:546
  18.5 0.1 add_select_fusion.1
  18.6 2.5 %collective-permute-start.3 = (f32[2,24,128]{2,1,0:T(8,128)S(1)}, f32[2,24,128]{2,1,0:T(8,128)S(1)}, u32[]{:S(2)}, u32[]{:S(2)}) collective-permute-start(f32[2,24,128]{2,1,0:T(8,128)S(1)} %add_select_fusion.1), channel_id=1, source_target_pairs={{0,4},{1,5},{2,6},{3,7},{4,0},{5,1},{6,2},{7,3},{8,12},{9,13},{10,... | collective-permute-start | bytes 73736 | tf_op jit(solution)/shard_map/ppermute | solution.py:546
  21.0 1.2 %collective-permute-done.3 = f32[2,24,128]{2,1,0:T(8,128)S(1)} collective-permute-done((f32[2,24,128]{2,1,0:T(8,128)S(1)}, f32[2,24,128]{2,1,0:T(8,128)S(1)}, u32[]{:S(2)}, u32[]{:S(2)}) %collective-permute-start.3) | collective-permute-done | bytes 24608 | tf_op jit(solution)/shard_map/ppermute | solution.py:546
  22.3 0.1 add_select_fusion.ends_ref
  22.3 2.3 %collective-permute-start.4 = (f32[2,24,128]{2,1,0:T(8,128)S(1)}, f32[2,24,128]{2,1,0:T(8,128)S(1)}, u32[]{:S(2)}, u32[]{:S(2)}) collective-permute-start(f32[2,24,128]{2,1,0:T(8,128)S(1)} %add_select_fusion.ends_ref), channel_id=1, source_target_pairs={{0,1},{1,0},{2,3},{3,2},{4,5},{5,4},{6,7},{7,6},{8,9},{9,8},{10,11... | collective-permute-start | bytes 73736 | tf_op jit(solution)/shard_map/ppermute | solution.py:550
  24.6 2.5 %gates.1 = (f32[12,3,4,32,128]{4,3,2,1,0:T(8,128)}, f32[10,16,128]{2,1,0:T(8,128)S(1)}) custom-call(f32[2,24,128]{2,1,0:T(8,128)S(1)} %add_select_fusion.ends_ref, f32[24,128]{1,0:T(8,128)S(1)} %get-tuple-element.22.par_ref, f32[4,24,32,128]{3,2,1,0:T(8,128)S(1)} %bitcast.3), custom_call_target="tpu_custom_call" | custom-call | flops 16777216 | bytes 8388608 | tf_op jit(solution)/shard_map/gates/pallas_call | solution.py:554
  27.1 0.0 collective-permute-done.4
  27.1 3.6 %collective-permute-start.5 = (f32[2,24,128]{2,1,0:T(8,128)S(1)}, f32[2,24,128]{2,1,0:T(8,128)S(1)}, u32[]{:S(2)}, u32[]{:S(2)}) collective-permute-start(f32[2,24,128]{2,1,0:T(8,128)S(1)} %add.14), channel_id=1, source_target_pairs={{0,8},{8,0},{1,9},{9,1},{2,10},{10,2},{3,11},{11,3},{4,12},{12,4},... | collective-permute-start | bytes 73736 | tf_op jit(solution)/shard_map/ppermute | solution.py:573
  30.8 1.1 %rest.1 = f32[12,3,4,32,128]{4,3,2,1,0:T(8,128)} custom-call(f32[10,16,128]{2,1,0:T(8,128)S(1)} %get-tuple-element.25.w_ref, f32[4,24,32,128]{3,2,1,0:T(8,128)S(1)} %bitcast.4, f32[12,3,4,32,128]{4,3,2,1,0:T(8,128)} %get-tuple-element.26.before_ref), custom_call_target="tpu_custom_call", output_to_operand_aliasing={{}: (2, {})} | custom-call | flops 4194304 | bytes 2097152 | tf_op jit(solution)/shard_map/rest/pallas_call | solution.py:574
  31.9 0.0 collective-permute-done.5
  31.9 0.7 %traces.1 = f32[12,3,256]{2,1,0:T(4,128)} custom-call(f32[10,16,128]{2,1,0:T(8,128)S(1)} %get-tuple-element.25.w_ref, f32[2,24,128]{2,1,0:T(8,128)S(1)} %add.15.sel_ref), custom_call_target="tpu_custom_call" | custom-call | tf_op jit(solution)/shard_map/traces/pallas_call | solution.py:591
  (3 shorter events, 0.0 us)
Async XLA Ops:
  0.6 0.9 %copy-start = (f32[4,64,128]{2,1,0:T(8,128)S(1)}, f32[4,64,128]{2,1,0:T(8,128)}, u32[]{:S(2)}) copy-start(f32[4,64,128]{2,1,0:T(8,128)} %cond_hbm.1) | copy-start | bytes 393220
  2.9 8.2 %collective-permute-start = (f32[352,128]{1,0:T(8,128)S(1)}, f32[352,128]{1,0:T(8,128)S(1)}, u32[]{:S(2)}, u32[]{:S(2)}) collective-permute-start(f32[352,128]{1,0:T(8,128)S(1)} %get-tuple-element.18), channel_id=1, source_target_pairs={{0,1},{1,0},{2,3},{3,2},{4,5},{5,4},{6,7},{7,6},{8,9},{9,8},{10,11... | collective-permute-start | bytes 540680 | tf_op jit(solution)/shard_map/ppermute | solution.py:504
  5.0 6.0 %collective-permute-start.1 = (f32[352,128]{1,0:T(8,128)S(1)}, f32[352,128]{1,0:T(8,128)S(1)}, u32[]{:S(2)}, u32[]{:S(2)}) collective-permute-start(f32[352,128]{1,0:T(8,128)S(1)} %get-tuple-element.19), channel_id=1, source_target_pairs={{1,2},{3,4},{5,6},{2,1},{4,3},{6,5},{9,10},{11,12},{13,14},{10,9},... | collective-permute-start | bytes 540680 | tf_op jit(solution)/shard_map/ppermute | solution.py:503
  5.7 0.7 %copy-start.1 = (f32[12,8]{0,1:T(8,128)S(1)}, f32[12,8]{0,1:T(8,128)}, u32[]{:S(2)}) copy-start(f32[12,8]{0,1:T(8,128)} %param.8) | copy-start | bytes 1156
  6.4 0.7 %copy-start.2 = (s32[256]{0:T(256)S(1)}, s32[256]{0:T(256)}, u32[]{:S(2)}) copy-start(s32[256]{0:T(256)} %rec_ref.1) | copy-start | bytes 3076
  7.1 0.7 %copy-start.3 = (f32[8]{0:T(128)S(1)}, f32[8]{0:T(128)}, u32[]{:S(2)}) copy-start(f32[8]{0:T(128)} %param.7) | copy-start | bytes 100
  14.2 4.3 %collective-permute-start.2 = (f32[2,24,128]{2,1,0:T(8,128)S(1)}, f32[2,24,128]{2,1,0:T(8,128)S(1)}, u32[]{:S(2)}, u32[]{:S(2)}) collective-permute-start(f32[2,24,128]{2,1,0:T(8,128)S(1)} %get-tuple-element.21), channel_id=1, source_target_pairs={{0,2},{1,3},{2,0},{3,1},{4,6},{5,7},{6,4},{7,5},{8,10},{9,11},{10,... | collective-permute-start | bytes 73736 | tf_op jit(solution)/shard_map/ppermute | solution.py:546
  18.6 3.7 %collective-permute-start.3 = (f32[2,24,128]{2,1,0:T(8,128)S(1)}, f32[2,24,128]{2,1,0:T(8,128)S(1)}, u32[]{:S(2)}, u32[]{:S(2)}) collective-permute-start(f32[2,24,128]{2,1,0:T(8,128)S(1)} %add_select_fusion.1), channel_id=1, source_target_pairs={{0,4},{1,5},{2,6},{3,7},{4,0},{5,1},{6,2},{7,3},{8,12},{9,13},{10,... | collective-permute-start | bytes 73736 | tf_op jit(solution)/shard_map/ppermute | solution.py:546
  22.3 4.8 %collective-permute-start.4 = (f32[2,24,128]{2,1,0:T(8,128)S(1)}, f32[2,24,128]{2,1,0:T(8,128)S(1)}, u32[]{:S(2)}, u32[]{:S(2)}) collective-permute-start(f32[2,24,128]{2,1,0:T(8,128)S(1)} %add_select_fusion.ends_ref), channel_id=1, source_target_pairs={{0,1},{1,0},{2,3},{3,2},{4,5},{5,4},{6,7},{7,6},{8,9},{9,8},{10,11... | collective-permute-start | bytes 73736 | tf_op jit(solution)/shard_map/ppermute | solution.py:550
  27.1 4.8 %collective-permute-start.5 = (f32[2,24,128]{2,1,0:T(8,128)S(1)}, f32[2,24,128]{2,1,0:T(8,128)S(1)}, u32[]{:S(2)}, u32[]{:S(2)}) collective-permute-start(f32[2,24,128]{2,1,0:T(8,128)S(1)} %add.14), channel_id=1, source_target_pairs={{0,8},{8,0},{1,9},{9,1},{2,10},{10,2},{3,11},{11,3},{4,12},{12,4},... | collective-permute-start | bytes 73736 | tf_op jit(solution)/shard_map/ppermute | solution.py:573

commit v2 on v1

--- a/solution.py
+++ b/solution.py
@@ -105,27 +105,18 @@
     return from_front(jnp.where(rows_of(last) < 2, pltpu.roll(tiles[at], 2, 0), last), core)
 
 
-def send_kernel(cond_hbm, src_hbm, first_ref, second_ref, cond_out, field_out, ends_ref, cond_ref, src_ref, sems):
+def send_kernel(all_ref, first_ref, second_ref, cond_out, field_out, ends_ref):
     core = lax.axis_index("pole")
     odd = lax.rem(lax.axis_index("space"), 2)
-    layers, rows, _ = cond_ref.shape
+    _, layers, rows, _ = all_ref.shape
     half = rows // 2
     own, extra = own_rows(half, core), extra_rows(half, core)
     keep = part_keep(core)
-    copies = [pltpu.make_async_copy(cond_hbm, cond_ref, sems.at[0])] + [
-        pltpu.make_async_copy(src_hbm.at[c], src_ref.at[c], sems.at[1 + c]) for c in range(3)
-    ]
-    for copy in copies:
-        copy.start()
-    for copy in copies:
-        copy.wait()
-
     conds, fields = [], []
     for layer in range(layers):
-        cond = jnp.concatenate([cond_ref[layer, own, :], cond_ref[layer, extra, :] * keep], axis=0)
-        field = [
-            cond * jnp.concatenate([src_ref[c, layer, own, :], src_ref[c, layer, extra, :]], axis=0)
-            for c in range(3)
+        *field, cond = [
+            jnp.concatenate([all_ref[c, layer, own, :], all_ref[c, layer, extra, :] * keep], axis=0)
+            for c in range(4)
         ]
         cond_out[layer] = cond
         for c in range(3):
@@ -133,8 +124,8 @@
         conds.append(cond)
         fields.append(field)
 
-    top = jnp.max(jnp.max(cond_ref[...], axis=0), axis=0, keepdims=True)
-    low = jnp.max(-jnp.min(cond_ref[...], axis=0), axis=0, keepdims=True)
+    top = jnp.max(jnp.max(all_ref[3], axis=0), axis=0, keepdims=True)
+    low = jnp.max(-jnp.min(all_ref[3], axis=0), axis=0, keepdims=True)
     row = lax.broadcasted_iota(jnp.int32, (TILE, 128), 0)
     ends = jnp.where(row == 0, top, low)
     ends_ref[...] = ends
@@ -488,16 +479,11 @@
             jax.ShapeDtypeStruct((layers, 3, half + TILE, depth), f32),
             jax.ShapeDtypeStruct((TILE, 128), f32),
         ],
-        in_specs=[hbm, hbm],
+        in_specs=[VMEM],
         out_specs=[VMEM] * 5,
-        scratch_shapes=[
-            pltpu.VMEM((layers, rows, depth), f32),
-            pltpu.VMEM((3, layers, rows, depth), f32),
-            pltpu.SemaphoreType.DMA((4,)),
-        ],
-        compiler_params=pltpu.CompilerParams(vmem_limit_bytes=53 * 1024 * 1024),
+        compiler_params=pltpu.CompilerParams(vmem_limit_bytes=48 * 1024 * 1024),
         name="send",
-    )(conductivity, source_field)
+    )(conductivity * jnp.pad(source_field, ((0, 1), (0, 0), (0, 0), (0, 0)), constant_values=1.0))
     far_pairs = [(i, i + 1) for i in range(1, size - 1, 2)]
     far_pairs = far_pairs + [(j, i) for i, j in far_pairs]
     second = lax.ppermute(second, "space", far_pairs)

time: 32.8 us -> 31.7 us (0.966)
  Pallas kernels: 12.1 us -> 10.6 us
  other arithmetic: 0.16 us -> 1.23 us
  local copies, waits for them, and re-layouts: 2.91 us -> 2.02 us
    pallas_call x1, Pallas kernels: 1.34 us -> 0.12 us  [per_device(): pl.pallas_call(send_kernel, out_shape=[message, message, jax.ShapeDtypeSt...]
    mul x0 -> x1, other arithmetic: none -> 1.06 us  [per_device(): conductivity * jnp.pad(source_field, ((0, 1), (0, 0), (0, 0), (0, 0)), co...]
    unnamed x8 -> x6, local copies, waits for them, and re-layouts: 2.91 us -> 2.02 us
    ppermute x1, starting transfers between devices: 2.28 us -> 1.87 us  [per_device(): other = lax.ppermute(sel, 'space', [(i, i ^ 1) for i in range(size)])]
    ppermute x2, starting transfers between devices: 5.56 us -> 5.93 us  [per_device(): other = lax.ppermute(sel, 'space', [(i, i ^ stride) for i in range(size)])]
  transfers between devices with their start and end apart: 6 -> 6, of which waited for: 2 -> 2; matrix products, arithmetic and copies ran while one was open for 0% -> 0% of each run, Pallas kernels for 21% -> 22%
where the time goes in v2:
time: 31.7 us; the launch traced here: 31.5 us
  starting transfers between devices  14.5 us (46%)
  Pallas kernels  10.6 us (33%)
  waiting for transfers between devices  2.44 us (8%)
  local copies, waits for them, and re-layouts  2.02 us (6%)
  other arithmetic  1.23 us (4%)
  between operations  0.71 us (2%)
    ppermute x2, starting transfers between devices, per_device(): other = lax.ppermute(sel, 'space', [(i, i ^ stride) for i in range(size)])  5.93 us
    ppermute x1, starting transfers between devices, per_device(): other = lax.ppermute(sel, 'pole', [(0, 1), (1, 0)])  3.93 us
    pallas_call x1, Pallas kernels, per_device(): pl.pallas_call(functools.partial(list_kernel, layers=layers, rows=rows, d...  3.31 us
    pallas_call x1, Pallas kernels, per_device(): pl.pallas_call(basis_kernel, out_shape=[jax.ShapeDtypeStruct((layers * SL...  2.88 us
    pallas_call x1, Pallas kernels, per_device(): pl.pallas_call(functools.partial(gate_kernel, poles=poles), grid=(early,)...  2.49 us
    ppermute x2, waiting for transfers between devices, per_device(): other = lax.ppermute(sel, 'space', [(i, i ^ stride) for i in range(size)])  2.43 us
    ppermute x1, starting transfers between devices, per_device(): first = lax.ppermute(first, 'space', [(i, i ^ 1) for i in range(size)])  2.14 us
    unnamed x6, local copies, waits for them, and re-layouts  2.02 us
  transfers between devices with their start and end apart: 6, of which 2 were waited for; matrix products, arithmetic and copies ran while one was open for 0% of the time, Pallas kernels for 22%

profile of v2, /device:TPU:1, one launch (start us, length us, event | category | flops | bytes accessed | tf_op | source)
XLA Modules:
  0.0 31.5 jit_solution(10011842865482616755)
XLA Ops:
  0.6 1.1 %pad_multiply_fusion.all_ref = f32[4,4,64,128]{3,2,1,0:T(8,128)S(1)} fusion(f32[3,4,64,128]{3,2,1,0:T(8,128)} %param.6, f32[4,64,128]{2,1,0:T(8,128)} %param.5), kind=kLoop, calls=%fused_computation | loop fusion | flops 131072 | bytes 1048576 | tf_op jit(solution)/shard_map/mul | solution.py:486
  1.7 0.1 send.1
  1.8 2.1 %collective-permute-start = (f32[352,128]{1,0:T(8,128)S(1)}, f32[352,128]{1,0:T(8,128)S(1)}, u32[]{:S(2)}, u32[]{:S(2)}) collective-permute-start(f32[352,128]{1,0:T(8,128)S(1)} %get-tuple-element.18), channel_id=1, source_target_pairs={{0,1},{1,0},{2,3},{3,2},{4,5},{5,4},{6,7},{7,6},{8,9},{9,8},{10,11... | collective-permute-start | bytes 540680 | tf_op jit(solution)/shard_map/ppermute | solution.py:490
  4.0 0.7 %collective-permute-start.1 = (f32[352,128]{1,0:T(8,128)S(1)}, f32[352,128]{1,0:T(8,128)S(1)}, u32[]{:S(2)}, u32[]{:S(2)}) collective-permute-start(f32[352,128]{1,0:T(8,128)S(1)} %get-tuple-element.19), channel_id=1, source_target_pairs={{1,2},{3,4},{5,6},{2,1},{4,3},{6,5},{9,10},{11,12},{13,14},{10,9},... | collective-permute-start | bytes 540680 | tf_op jit(solution)/shard_map/ppermute | solution.py:489
  4.6 0.0 copy-start
  4.6 0.7 %copy-done = f32[12,8]{0,1:T(8,128)S(1)} copy-done((f32[12,8]{0,1:T(8,128)S(1)}, f32[12,8]{0,1:T(8,128)}, u32[]{:S(2)}) %copy-start) | copy-done | bytes 408
  5.3 0.0 copy-start.1
  5.3 0.7 %copy-done.1 = s32[256]{0:T(256)S(1)} copy-done((s32[256]{0:T(256)S(1)}, s32[256]{0:T(256)}, u32[]{:S(2)}) %copy-start.1) | copy-done | bytes 1048
  6.0 0.0 copy-start.2
  6.0 0.7 %copy-done.2 = f32[8]{0:T(128)S(1)} copy-done((f32[8]{0:T(128)S(1)}, f32[8]{0:T(128)}, u32[]{:S(2)}) %copy-start.2) | copy-done | bytes 56
  6.7 3.3 %owned.1 = (s32[257]{0:T(512)S(1)}, f32[24,128]{1,0:T(8,128)S(1)}) custom-call(s32[256]{0:T(256)S(1)} %copy-done.1, f32[1,8]{1,0:T(1,128)S(1)} %bitcast.6, f32[8,12]{1,0:T(8,128)S(1)} %bitcast.5), custom_call_target="tpu_custom_call" | custom-call | tf_op jit(solution)/shard_map/owned/pallas_call | solution.py:492
  10.0 0.0 collective-permute-done.first_ref
  10.0 0.0 collective-permute-done.1.second_ref
  10.0 2.9 %basis.1 = (f32[3072,128]{1,0:T(8,128)S(1)}, f32[2,24,128]{2,1,0:T(8,128)S(1)}) custom-call(f32[4,40,128]{2,1,0:T(8,128)S(1)} %get-tuple-element.15.cond_ref, f32[4,3,40,128]{3,2,1,0:T(8,128)S(1)} %get-tuple-element.16.field_ref, f32[8,128]{1,0:T(8,128)S(1)} %get-tuple-element.17.ends_ref, f32[352,128]{1,0:T(8,128)S(1)} %collective-permute-done.first_ref, ...), custom_call_target="tpu_custom_call" | custom-call | tf_op jit(solution)/shard_map/basis/pallas_call | solution.py:508
  12.9 3.2 %collective-permute-start.2 = (f32[2,24,128]{2,1,0:T(8,128)S(1)}, f32[2,24,128]{2,1,0:T(8,128)S(1)}, u32[]{:S(2)}, u32[]{:S(2)}) collective-permute-start(f32[2,24,128]{2,1,0:T(8,128)S(1)} %get-tuple-element.21), channel_id=1, source_target_pairs={{0,2},{1,3},{2,0},{3,1},{4,6},{5,7},{6,4},{7,5},{8,10},{9,11},{10,... | collective-permute-start | bytes 73736 | tf_op jit(solution)/shard_map/ppermute | solution.py:532
  16.1 1.2 %collective-permute-done.2 = f32[2,24,128]{2,1,0:T(8,128)S(1)} collective-permute-done((f32[2,24,128]{2,1,0:T(8,128)S(1)}, f32[2,24,128]{2,1,0:T(8,128)S(1)}, u32[]{:S(2)}, u32[]{:S(2)}) %collective-permute-start.2) | collective-permute-done | bytes 24608 | tf_op jit(solution)/shard_map/ppermute | solution.py:532
  17.3 0.1 add_select_fusion.1
  17.4 2.7 %collective-permute-start.3 = (f32[2,24,128]{2,1,0:T(8,128)S(1)}, f32[2,24,128]{2,1,0:T(8,128)S(1)}, u32[]{:S(2)}, u32[]{:S(2)}) collective-permute-start(f32[2,24,128]{2,1,0:T(8,128)S(1)} %add_select_fusion.1), channel_id=1, source_target_pairs={{0,4},{1,5},{2,6},{3,7},{4,0},{5,1},{6,2},{7,3},{8,12},{9,13},{10,... | collective-permute-start | bytes 73736 | tf_op jit(solution)/shard_map/ppermute | solution.py:532
  20.1 1.2 %collective-permute-done.3 = f32[2,24,128]{2,1,0:T(8,128)S(1)} collective-permute-done((f32[2,24,128]{2,1,0:T(8,128)S(1)}, f32[2,24,128]{2,1,0:T(8,128)S(1)}, u32[]{:S(2)}, u32[]{:S(2)}) %collective-permute-start.3) | collective-permute-done | bytes 24608 | tf_op jit(solution)/shard_map/ppermute | solution.py:532
  21.3 0.1 add_select_fusion.ends_ref
  21.4 1.9 %collective-permute-start.4 = (f32[2,24,128]{2,1,0:T(8,128)S(1)}, f32[2,24,128]{2,1,0:T(8,128)S(1)}, u32[]{:S(2)}, u32[]{:S(2)}) collective-permute-start(f32[2,24,128]{2,1,0:T(8,128)S(1)} %add_select_fusion.ends_ref), channel_id=1, source_target_pairs={{0,1},{1,0},{2,3},{3,2},{4,5},{5,4},{6,7},{7,6},{8,9},{9,8},{10,11... | collective-permute-start | bytes 73736 | tf_op jit(solution)/shard_map/ppermute | solution.py:536
  23.3 2.5 %gates.1 = (f32[12,3,4,32,128]{4,3,2,1,0:T(8,128)}, f32[10,16,128]{2,1,0:T(8,128)S(1)}) custom-call(f32[2,24,128]{2,1,0:T(8,128)S(1)} %add_select_fusion.ends_ref, f32[24,128]{1,0:T(8,128)S(1)} %get-tuple-element.22.par_ref, f32[4,24,32,128]{3,2,1,0:T(8,128)S(1)} %bitcast.3), custom_call_target="tpu_custom_call" | custom-call | flops 16777216 | bytes 8388608 | tf_op jit(solution)/shard_map/gates/pallas_call | solution.py:540
  25.8 0.0 collective-permute-done.4
  25.8 3.9 %collective-permute-start.5 = (f32[2,24,128]{2,1,0:T(8,128)S(1)}, f32[2,24,128]{2,1,0:T(8,128)S(1)}, u32[]{:S(2)}, u32[]{:S(2)}) collective-permute-start(f32[2,24,128]{2,1,0:T(8,128)S(1)} %add.16), channel_id=1, source_target_pairs={{0,8},{8,0},{1,9},{9,1},{2,10},{10,2},{3,11},{11,3},{4,12},{12,4},... | collective-permute-start | bytes 73736 | tf_op jit(solution)/shard_map/ppermute | solution.py:559
  29.7 1.1 %rest.1 = f32[12,3,4,32,128]{4,3,2,1,0:T(8,128)} custom-call(f32[10,16,128]{2,1,0:T(8,128)S(1)} %get-tuple-element.25.w_ref, f32[4,24,32,128]{3,2,1,0:T(8,128)S(1)} %bitcast.4, f32[12,3,4,32,128]{4,3,2,1,0:T(8,128)} %get-tuple-element.26.before_ref), custom_call_target="tpu_custom_call", output_to_operand_aliasing={{}: (2, {})} | custom-call | flops 4194304 | bytes 2097152 | tf_op jit(solution)/shard_map/rest/pallas_call | solution.py:560
  30.8 0.0 collective-permute-done.5
  30.8 0.7 %traces.1 = f32[12,3,256]{2,1,0:T(4,128)} custom-call(f32[10,16,128]{2,1,0:T(8,128)S(1)} %get-tuple-element.25.w_ref, f32[2,24,128]{2,1,0:T(8,128)S(1)} %add.17.sel_ref), custom_call_target="tpu_custom_call" | custom-call | tf_op jit(solution)/shard_map/traces/pallas_call | solution.py:577
  (3 shorter events, 0.0 us)
Async XLA Ops:
  1.8 8.2 %collective-permute-start = (f32[352,128]{1,0:T(8,128)S(1)}, f32[352,128]{1,0:T(8,128)S(1)}, u32[]{:S(2)}, u32[]{:S(2)}) collective-permute-start(f32[352,128]{1,0:T(8,128)S(1)} %get-tuple-element.18), channel_id=1, source_target_pairs={{0,1},{1,0},{2,3},{3,2},{4,5},{5,4},{6,7},{7,6},{8,9},{9,8},{10,11... | collective-permute-start | bytes 540680 | tf_op jit(solution)/shard_map/ppermute | solution.py:490
  4.0 6.0 %collective-permute-start.1 = (f32[352,128]{1,0:T(8,128)S(1)}, f32[352,128]{1,0:T(8,128)S(1)}, u32[]{:S(2)}, u32[]{:S(2)}) collective-permute-start(f32[352,128]{1,0:T(8,128)S(1)} %get-tuple-element.19), channel_id=1, source_target_pairs={{1,2},{3,4},{5,6},{2,1},{4,3},{6,5},{9,10},{11,12},{13,14},{10,9},... | collective-permute-start | bytes 540680 | tf_op jit(solution)/shard_map/ppermute | solution.py:489
  4.6 0.7 %copy-start = (f32[12,8]{0,1:T(8,128)S(1)}, f32[12,8]{0,1:T(8,128)}, u32[]{:S(2)}) copy-start(f32[12,8]{0,1:T(8,128)} %param.8) | copy-start | bytes 1156
  5.3 0.7 %copy-start.1 = (s32[256]{0:T(256)S(1)}, s32[256]{0:T(256)}, u32[]{:S(2)}) copy-start(s32[256]{0:T(256)} %rec_ref.1) | copy-start | bytes 3076
  6.0 0.7 %copy-start.2 = (f32[8]{0:T(128)S(1)}, f32[8]{0:T(128)}, u32[]{:S(2)}) copy-start(f32[8]{0:T(128)} %param.7) | copy-start | bytes 100
  12.9 4.4 %collective-permute-start.2 = (f32[2,24,128]{2,1,0:T(8,128)S(1)}, f32[2,24,128]{2,1,0:T(8,128)S(1)}, u32[]{:S(2)}, u32[]{:S(2)}) collective-permute-start(f32[2,24,128]{2,1,0:T(8,128)S(1)} %get-tuple-element.21), channel_id=1, source_target_pairs={{0,2},{1,3},{2,0},{3,1},{4,6},{5,7},{6,4},{7,5},{8,10},{9,11},{10,... | collective-permute-start | bytes 73736 | tf_op jit(solution)/shard_map/ppermute | solution.py:532
  17.4 3.9 %collective-permute-start.3 = (f32[2,24,128]{2,1,0:T(8,128)S(1)}, f32[2,24,128]{2,1,0:T(8,128)S(1)}, u32[]{:S(2)}, u32[]{:S(2)}) collective-permute-start(f32[2,24,128]{2,1,0:T(8,128)S(1)} %add_select_fusion.1), channel_id=1, source_target_pairs={{0,4},{1,5},{2,6},{3,7},{4,0},{5,1},{6,2},{7,3},{8,12},{9,13},{10,... | collective-permute-start | bytes 73736 | tf_op jit(solution)/shard_map/ppermute | solution.py:532
  21.4 4.4 %collective-permute-start.4 = (f32[2,24,128]{2,1,0:T(8,128)S(1)}, f32[2,24,128]{2,1,0:T(8,128)S(1)}, u32[]{:S(2)}, u32[]{:S(2)}) collective-permute-start(f32[2,24,128]{2,1,0:T(8,128)S(1)} %add_select_fusion.ends_ref), channel_id=1, source_target_pairs={{0,1},{1,0},{2,3},{3,2},{4,5},{5,4},{6,7},{7,6},{8,9},{9,8},{10,11... | collective-permute-start | bytes 73736 | tf_op jit(solution)/shard_map/ppermute | solution.py:536
  25.8 5.1 %collective-permute-start.5 = (f32[2,24,128]{2,1,0:T(8,128)S(1)}, f32[2,24,128]{2,1,0:T(8,128)S(1)}, u32[]{:S(2)}, u32[]{:S(2)}) collective-permute-start(f32[2,24,128]{2,1,0:T(8,128)S(1)} %add.16), channel_id=1, source_target_pairs={{0,8},{8,0},{1,9},{9,1},{2,10},{10,2},{3,11},{11,3},{4,12},{12,4},... | collective-permute-start | bytes 73736 | tf_op jit(solution)/shard_map/ppermute | solution.py:559

commit v3 on v2

--- a/solution.py
+++ b/solution.py
@@ -155,34 +155,7 @@
             write(second_ref)
 
 
-def list_kernel(rec_ref, shifts_ref, res_ref, list_ref, par_ref, square, *, layers, rows, depth):
-    core = lax.axis_index("pole")
-    base = lax.axis_index("space") * layers
-    half = rows // 2
-    total = rec_ref.shape[0]
-
-    bits = bits_of(total)
-
-    def step(at, count):
-        line, z = split(rec_ref[at], depth)
-        x, y = split(line, rows)
-        x, y = x - base, y - core * half
-        owned = (x >= 0) & (x < layers) & (y >= 0) & (y < half)
-        start = x * (SLOTS * half) + y
-        turn = (at - z) & 127
-        list_ref[count] = (((start << 7) | turn) << bits) | at
-        return count + owned.astype(jnp.int32)
-
-    list_ref[total] = lax.fori_loop(0, total, step, jnp.int32(0), unroll=8)
-    poles, gates = res_ref.shape
-    square[...] = jnp.zeros_like(square)
-    square[:poles, :gates] = res_ref[...]
-    par_ref[...] = jnp.zeros_like(par_ref)
-    par_ref[TILE : TILE + gates, :poles] = square[...].T[:gates, :poles]
-    par_ref[:1, :poles] = shifts_ref[...]
-
-
-def curl_curl(get_u, get, layers, put, half, trimmed=False):
+def curl_curl(get_u, get, layers, put):
     first = layers[0]
     u_y, u_z = get_u(first - 1)
     _, g, e = get(first, (1, 2))
@@ -200,66 +173,93 @@
         put(layer, (out_x, out_y, out_z))
 
 
+def own_kernel(code_ref, cond_ref, field_ref, list_ref, sig_ref, one_ref, mixed_ref, twice_ref, t11, t22):
+    layers, reach, depth = cond_ref.shape
+    blank = jnp.zeros((reach, depth), jnp.float32)
+    for layer in range(layers):
+        moved = cond_ref[layer] - MID
+        sig_ref[layer] = moved
+        for c in range(3):
+            once = moved * field_ref[layer, c]
+            t11[layer, c] = once
+            t22[layer, c] = moved * once
+
+    def apply(src, out):
+        def get(layer, which):
+            if layer == layers:
+                return [blank] * 3
+            return [src[layer, c] if c in which else None for c in range(3)]
+
+        def put(layer, values):
+            for c in range(3):
+                out[layer, c] = values[c]
+
+        curl_curl(lambda layer: (blank, blank), get, list(range(layers)), put)
+
+    apply(field_ref, one_ref)
+    apply(t11, mixed_ref)
+    apply(t22, twice_ref)
+
+    total = code_ref.shape[0]
+
+    def step(at, count):
+        code = code_ref[at]
+        list_ref[count] = code
+        return count + (code >= 0).astype(jnp.int32)
+
+    list_ref[total] = lax.fori_loop(0, total, step, jnp.int32(0), unroll=8)
+
+
 def basis_kernel(
-    cond_ref, field_ref, ends_ref, first_ref, second_ref, list_hbm,
+    field_ref, sig_ref, one_ref, mixed_ref, twice_ref, ends_ref, first_ref, second_ref, list_hbm,
     bas_ref, sel_ref,
-    sig, low3, high3, t00, t10, t11, t20, t21, t22, list_ref, list_sem,
+    sig, low3, high3, t00, t11, t10, t20, t21, list_ref, list_sem,
 ):
     core = lax.axis_index("pole")
     place = lax.axis_index("space")
     odd = lax.rem(place, 2)
-    layers, reach, depth = cond_ref.shape
+    layers, _, reach, depth = field_ref.shape
     half = reach - TILE
     keep = part_keep(core)
     list_copy = pltpu.make_async_copy(list_hbm, list_ref, list_sem)
     list_copy.start()
     low_ok = (place > 0).astype(jnp.float32)
     high_ok = (place < lax.axis_size("space") - 1).astype(jnp.float32)
-
-    def received(upward, at):
-        part = pl.ds(at * half, half)
+    first, last = 2, layers + 1
+    inner = list(range(first, last + 1))
+
+    def received(upward, start, size):
+        part = pl.ds(start, size)
         from_first = odd == 1 if upward else odd == 0
         return jnp.where(from_first, first_ref[part, :], second_ref[part, :])
 
-    def received_tile(upward, at):
-        part = pl.ds(10 * half + at * TILE, TILE)
-        from_first = odd == 1 if upward else odd == 0
-        return jnp.where(from_first, first_ref[part, :], second_ref[part, :])
-
-    for layer in range(layers):
-        moved = cond_ref[layer] - MID
-        sig[layer + 2] = moved
-        for c in range(3):
-            field = field_ref[layer, c]
-            t00[layer + 2, c] = field
-            t11[layer + 2, c] = moved * field
     for upward in (True, False):
-        tiles = [received_tile(upward, at) for at in range(4)]
+        tiles = [received(upward, 10 * half + at * TILE, TILE) for at in range(4)]
+        blocks = [received(upward, at * half, half) for at in range(10)]
+        near = [
+            jnp.concatenate([blocks[at], unpack_near(tiles, at, core)], axis=0) for at in range(8)
+        ]
         for distance in (1, 2):
-            slot = 2 - distance if upward else layers + 1 + distance
+            slot = first - distance if upward else last + distance
             base = (distance - 1) * 4
-            moved = jnp.concatenate(
-                [received(upward, base + 3), unpack_near(tiles, base + 3, core)], axis=0
-            ) - MID
+            moved = near[base + 3] - MID
             sig[slot] = moved
             for c in range(3):
-                field = jnp.concatenate(
-                    [received(upward, base + c), unpack_near(tiles, base + c, core)], axis=0
-                )
-                t00[slot, c] = field
-                t11[slot, c] = moved * field
+                t00[slot, c] = near[base + c]
+                t11[slot, c] = moved * near[base + c]
         far = low3 if upward else high3
         for at in range(2):
-            far[at] = jnp.concatenate(
-                [received(upward, 8 + at), unpack_far(tiles, at, core)], axis=0
-            )
-
-    def sums(ref):
-        def get_u(slot):
-            f, g, e = ref[slot, 0], ref[slot, 1], ref[slot, 2]
-            return g + (sub_next(f) - f), e + (lane_next(f) - f)
-
-        return get_u
+            far[at] = jnp.concatenate([blocks[8 + at], unpack_far(tiles, at, core)], axis=0)
+    for slot in (first, last):
+        for c in range(3):
+            t11[slot, c] = sig_ref[slot - first] * field_ref[slot - first, c]
+
+    def get_b(slot, which):
+        if slot > last + 2:
+            return None, high3[0], high3[1]
+        if slot in inner:
+            return [field_ref[slot - first, c] if c in which else None for c in range(3)]
+        return [t00[slot, c] if c in which else None for c in range(3)]
 
     def reader(ref):
         def get(slot, which):
@@ -267,63 +267,93 @@
 
         return get
 
+    def sums(get):
+        def get_u(slot):
+            if slot < 0:
+                return low3[0], low3[1]
+            f, g, e = get(slot, (0, 1, 2))
+            return g + (sub_next(f) - f), e + (lane_next(f) - f)
+
+        return get_u
+
     def inside(slot, value):
         value = jnp.concatenate([value[:half], value[half:] * keep], axis=0)
-        if slot < 2:
+        if slot < first:
             return value * low_ok
-        if slot > layers + 1:
+        if slot > last:
             return value * high_ok
         return value
 
-    def get_b(slot, which):
-        if slot > layers + 3:
-            return None, high3[0], high3[1]
-        return [t00[slot, c] if c in which else None for c in range(3)]
+    def completed(part_ref, slot, get):
+        out = [part_ref[slot - first, c] for c in range(3)]
+        if slot == first:
+            u_y, u_z = sums(get)(slot - 1)
+            out[1] = out[1] - u_y
+            out[2] = out[2] - u_z
+        if slot == last:
+            _, g, e = get(slot + 1, (1, 2))
+            out[0] = out[0] + (g - sub_prev(g)) + (e - lane_prev(e, 0.0))
+            out[1] = out[1] - g
+            out[2] = out[2] - e
+        return out
 
     def put_10(slot, out):
         for c in range(3):
             t10[slot, c] = inside(slot, out[c])
 
-    curl_curl(lambda slot: (low3[0], low3[1]), get_b, list(range(layers + 4)), put_10, half)
+    def put_21(slot, out):
+        moved = sig_ref[slot - first] if slot in inner else sig[slot]
+        for c in range(3):
+            t21[slot, c] = inside(slot, out[c]) + moved * t10[slot, c]
 
     def put_20(slot, out):
         for c in range(3):
             t20[slot, c] = inside(slot, out[c])
 
-    def put_21(slot, out):
-        for c in range(3):
-            t21[slot, c] = inside(slot, out[c]) + sig[slot] * t10[slot, c]
-            t22[slot, c] = sig[slot] * t11[slot, c]
-
-    middle = list(range(1, layers + 3))
-    curl_curl(sums(t10), reader(t10), middle, put_20, half)
-    curl_curl(sums(t11), reader(t11), middle, put_21, half)
+    curl_curl(sums(get_b), get_b, [0, 1], put_10)
+    curl_curl(sums(get_b), get_b, [last + 1, last + 2], put_10)
+    for slot in inner:
+        put_10(slot, completed(one_ref, slot, get_b))
+    get_11 = reader(t11)
+    curl_curl(sums(get_11), get_11, [first - 1], put_21)
+    curl_curl(sums(get_11), get_11, [last + 1], put_21)
+    for slot in inner:
+        put_21(slot, completed(mixed_ref, slot, get_11))
+    get_10 = reader(t10)
+    curl_curl(sums(get_10), get_10, list(range(first - 1, last + 2)), put_20)
 
     def store(word, slot, c, value):
-        base = ((slot - 2) * SLOTS + word * 3 + c) * half
+        base = ((slot - first) * SLOTS + word * 3 + c) * half
         bas_ref[base : base + half, :] = value
 
-    inner = list(range(2, layers + 2))
     for slot in inner:
         for c in range(3):
-            for word, ref in enumerate((t00, t10, t20, t21)):
+            store(0, slot, c, field_ref[slot - first, c, :half, :])
+            for word, ref in enumerate((t10, t20, t21), 1):
                 store(word, slot, c, ref[slot, c, :half, :])
-        base = ((slot - 2) * SLOTS + SIGMA) * half
-        bas_ref[base : base + half, :] = sig[slot, :half, :]
+        base = ((slot - first) * SLOTS + SIGMA) * half
+        bas_ref[base : base + half, :] = sig_ref[slot - first, :half, :]
 
     def put_3(word, before):
         def put(slot, out):
             for c in range(3):
                 value = out[c][:half]
                 if before is not None:
-                    value = value + sig[slot, :half, :] * before[slot, c, :half, :]
+                    moved = sig_ref[slot - first, :half, :]
+                    value = value + moved * before[slot, c, :half, :]
                 store(word, slot, c, value)
 
         return put
 
-    curl_curl(sums(t20), reader(t20), inner, put_3(4, None), half)
-    curl_curl(sums(t21), reader(t21), inner, put_3(5, t20), half)
-    curl_curl(sums(t22), reader(t22), inner, put_3(6, t21), half)
+    get_20, get_21 = reader(t20), reader(t21)
+    curl_curl(sums(get_20), get_20, inner, put_3(4, None))
+    curl_curl(sums(get_21), get_21, inner, put_3(5, t20))
+
+    def get_22(slot, which):
+        return [sig[slot] * t11[slot, c] if c in which else None for c in range(3)]
+
+    for slot in inner:
+        put_3(6, t21)(slot, completed(twice_ref, slot, get_22))
 
     groups = sel_ref.shape[0]
     lane = lax.broadcasted_iota(jnp.int32, (SLOTS, depth), 1)
@@ -489,18 +519,35 @@
     second = lax.ppermute(second, "space", far_pairs)
     first = lax.ppermute(first, "space", [(i, i ^ 1) for i in range(size)])
 
-    listed, params = pl.pallas_call(
-        functools.partial(list_kernel, layers=layers, rows=rows, depth=depth),
+    line, z = receivers // depth, receivers % depth
+    x = line // rows - lax.axis_index("space") * layers
+    y = line % rows - lax.axis_index("pole") * half
+    owned = (x >= 0) & (x < layers) & (y >= 0) & (y < half)
+    order = lax.iota(jnp.int32, count)
+    codes = (((x * (SLOTS * half) + y) << 7) | ((order - z) & 127)) << bits_of(count) | order
+    codes = jnp.where(owned, codes, -1)
+    params = jnp.pad(
+        jnp.concatenate([jnp.pad(shifts[None], ((0, TILE - 1), (0, 0))), residues]),
+        ((0, 16 - gates), (0, 128 - poles)),
+    )
+
+    own_shape = jax.ShapeDtypeStruct((layers, 3, half + TILE, depth), f32)
+    listed, own_sig, own_one, own_mixed, own_twice = pl.pallas_call(
+        own_kernel,
         out_shape=[
             jax.ShapeDtypeStruct((count + 1,), jnp.int32),
-            jax.ShapeDtypeStruct((TILE + 16, 128), f32),
+            jax.ShapeDtypeStruct((layers, half + TILE, depth), f32),
+            own_shape,
+            own_shape,
+            own_shape,
         ],
         in_specs=[SMEM, VMEM, VMEM],
-        out_specs=[SMEM, VMEM],
-        scratch_shapes=[pltpu.VMEM((TILE, 128), f32)],
+        out_specs=[SMEM] + [VMEM] * 4,
+        scratch_shapes=[pltpu.VMEM(own_shape.shape, f32)] * 2,
         compiler_params=PARAMS,
+        cost_estimate=pl.CostEstimate(flops=2**23, bytes_accessed=2**22, transcendentals=0),
         name="owned",
-    )(receivers, shifts.reshape(1, poles), residues.T)
+    )(codes, own_cond, own_field)
 
     def field(slots):
         return pltpu.VMEM((slots, 3, half + TILE, depth), f32)
@@ -511,19 +558,19 @@
             jax.ShapeDtypeStruct((layers * SLOTS * half, depth), f32),
             jax.ShapeDtypeStruct((groups, SLOTS, 128), f32),
         ],
-        in_specs=[VMEM] * 5 + [hbm],
+        in_specs=[VMEM] * 8 + [hbm],
         out_specs=[VMEM, VMEM],
         scratch_shapes=[
             pltpu.VMEM((layers + 4, half + TILE, depth), f32),
             pltpu.VMEM((2, half + TILE, depth), f32),
             pltpu.VMEM((2, half + TILE, depth), f32),
-            *[field(layers + 4) for _ in range(6)],
+            *[field(layers + 4) for _ in range(5)],
             pltpu.SMEM((count + 1,), jnp.int32),
             pltpu.SemaphoreType.DMA(()),
         ],
         compiler_params=PARAMS,
         name="basis",
-    )(own_cond, own_field, own_ends, first, second, listed)
+    )(own_field, own_sig, own_one, own_mixed, own_twice, own_ends, first, second, listed)
     basis = basis.reshape(layers, SLOTS, half, depth)
 
     is_end = lax.broadcasted_iota(jnp.int32, sel.shape, 1) >= ENDS

time: 31.7 us -> 30.4 us (0.959)
  local copies, waits for them, and re-layouts: 2.02 us -> 0.1 us
  Pallas kernels: 10.6 us -> 8.87 us
  starting transfers between devices: 14.5 us -> 15.6 us
  other arithmetic: 1.23 us -> 1.95 us
  waiting for transfers between devices: 2.44 us -> 2.8 us
    unnamed x6 -> x5, local copies, waits for them, and re-layouts: 2.02 us -> 0.09 us
    ppermute x2, starting transfers between devices: 5.93 us -> 7.32 us  [per_device(): other = lax.ppermute(sel, 'space', [(i, i ^ stride) for i in range(size)])]
    ppermute x1, starting transfers between devices: 1.87 us -> 0.7 us  [per_device(): other = lax.ppermute(sel, 'space', [(i, i ^ 1) for i in range(size)])]
    ppermute x1, starting transfers between devices: 3.93 us -> 4.82 us  [per_device(): other = lax.ppermute(sel, 'pole', [(0, 1), (1, 0)])]
    pallas_call x1, Pallas kernels: 2.88 us -> 1.99 us  [per_device(): pl.pallas_call(basis_kernel, out_shape=[jax.ShapeDtypeStruct((layers * SL...]
    pallas_call x1, Pallas kernels: 3.31 us -> 2.45 us  [per_device(): pl.pallas_call(own_kernel, out_shape=[jax.ShapeDtypeStruct((count + 1,),...]
    select_n x0 -> x1, other arithmetic: none -> 0.71 us  [per_device(): codes = jnp.where(owned, codes, -1)]
    ppermute x1, waiting for transfers between devices: 0.01 us -> 0.44 us  [per_device(): first = lax.ppermute(first, 'space', [(i, i ^ 1) for i in range(size)])]
  transfers between devices with their start and end apart: 6 -> 6, of which waited for: 2 -> 3; matrix products, arithmetic and copies ran while one was open for 0% -> 3% of each run, Pallas kernels for 22% -> 20%
where the time goes in v3:
time: 30.4 us; the launch traced here: 30.1 us
  starting transfers between devices  15.6 us (51%)
  Pallas kernels  8.87 us (29%)
  waiting for transfers between devices  2.8 us (9%)
  other arithmetic  1.95 us (6%)
  between operations  0.72 us (2%)
    ppermute x2, starting transfers between devices, per_device(): other = lax.ppermute(sel, 'space', [(i, i ^ stride) for i in range(size)])  7.32 us
    ppermute x1, starting transfers between devices, per_device(): other = lax.ppermute(sel, 'pole', [(0, 1), (1, 0)])  4.82 us
    pallas_call x1, Pallas kernels, per_device(): pl.pallas_call(functools.partial(gate_kernel, poles=poles), grid=(early,)...  2.52 us
    pallas_call x1, Pallas kernels, per_device(): pl.pallas_call(own_kernel, out_shape=[jax.ShapeDtypeStruct((count + 1,),...  2.45 us
    ppermute x2, waiting for transfers between devices, per_device(): other = lax.ppermute(sel, 'space', [(i, i ^ stride) for i in range(size)])  2.35 us
    ppermute x1, starting transfers between devices, per_device(): first = lax.ppermute(first, 'space', [(i, i ^ 1) for i in range(size)])  2.14 us
    pallas_call x1, Pallas kernels, per_device(): pl.pallas_call(basis_kernel, out_shape=[jax.ShapeDtypeStruct((layers * SL...  1.99 us
    pallas_call x1, Pallas kernels, per_device(): pl.pallas_call(functools.partial(rest_kernel, early=early), grid=(layers...  1.13 us
  transfers between devices with their start and end apart: 6, of which 3 were waited for; matrix products, arithmetic and copies ran while one was open for 3% of the time, Pallas kernels for 20%

profile of v3, /device:TPU:1, one launch (start us, length us, event | category | flops | bytes accessed | tf_op | source)
XLA Modules:
  0.0 30.1 jit_solution(9363809897146301422)
XLA Ops:
  0.6 0.0 copy-start
  0.6 0.0 copy-start.1
  0.7 1.1 %pad_multiply_fusion.all_ref = f32[4,4,64,128]{3,2,1,0:T(8,128)S(1)} fusion(f32[3,4,64,128]{3,2,1,0:T(8,128)} %param.6, f32[4,64,128]{2,1,0:T(8,128)} %param.5), kind=kLoop, calls=%fused_computation | loop fusion | flops 131072 | bytes 1048576 | tf_op jit(solution)/shard_map/mul | solution.py:516
  1.7 0.1 send.1
  1.9 2.1 %collective-permute-start = (f32[352,128]{1,0:T(8,128)S(1)}, f32[352,128]{1,0:T(8,128)S(1)}, u32[]{:S(2)}, u32[]{:S(2)}) collective-permute-start(f32[352,128]{1,0:T(8,128)S(1)} %get-tuple-element.25), channel_id=1, source_target_pairs={{0,1},{1,0},{2,3},{3,2},{4,5},{5,4},{6,7},{7,6},{8,9},{9,8},{10,11... | collective-permute-start | bytes 540680 | tf_op jit(solution)/shard_map/ppermute | solution.py:520
  4.0 0.7 %collective-permute-start.1 = (f32[352,128]{1,0:T(8,128)S(1)}, f32[352,128]{1,0:T(8,128)S(1)}, u32[]{:S(2)}, u32[]{:S(2)}) collective-permute-start(f32[352,128]{1,0:T(8,128)S(1)} %get-tuple-element.26), channel_id=1, source_target_pairs={{1,2},{3,4},{5,6},{2,1},{4,3},{6,5},{9,10},{11,12},{13,14},{10,9},... | collective-permute-start | bytes 540680 | tf_op jit(solution)/shard_map/ppermute | solution.py:519
  4.7 0.7 %and_select_fusion.1.code_ref = s32[256]{0:T(256)S(1)} fusion(s32[256]{0:T(256)} %param.9, s32[]{:T(128)S(6)} %mul.23, s32[]{:T(128)S(6)} %mul.22), kind=kLoop, calls=%fused_computation.6 | loop fusion | flops 14336 | bytes 2056 | tf_op jit(solution)/shard_map/jit(_where)/select_n | solution.py:528
  5.4 2.4 %owned.1 = (s32[257]{0:T(512)S(1)}, f32[4,40,128]{2,1,0:T(8,128)S(1)}, f32[4,3,40,128]{3,2,1,0:T(8,128)S(1)}, f32[4,3,40,128]{3,2,1,0:T(8,128)S(1)}, f32[4,3,40,128]{3,2,1,0:T(8,128)S(1)}) custom-call(s32[256]{0:T(256)S(1)} %and_select_fusion.1.code_ref, f32[4,40,128]{2,1,0:T(8,128)S(1)} %get-tuple-element.19.cond_ref, ...), custom_call_target="tpu_custom_call" | custom-call | flops 8388608 | bytes 4194304 | tf_op jit(solution)/shard_map/owned/pallas_call | solution.py:535
  7.8 0.4 %collective-permute-done.first_ref = f32[352,128]{1,0:T(8,128)S(1)} collective-permute-done((f32[352,128]{1,0:T(8,128)S(1)}, f32[352,128]{1,0:T(8,128)S(1)}, u32[]{:S(2)}, u32[]{:S(2)}) %collective-permute-start) | collective-permute-done | bytes 180256 | tf_op jit(solution)/shard_map/ppermute | solution.py:520
  8.3 0.0 collective-permute-done.1.second_ref
  8.3 2.0 %basis.1 = (f32[3072,128]{1,0:T(8,128)S(1)}, f32[2,24,128]{2,1,0:T(8,128)S(1)}) custom-call(f32[4,3,40,128]{3,2,1,0:T(8,128)S(1)} %get-tuple-element.18.field_ref, f32[4,40,128]{2,1,0:T(8,128)S(1)} %get-tuple-element.20.sig_ref, f32[4,3,40,128]{3,2,1,0:T(8,128)S(1)} %get-tuple-element.21.one_ref, f32[4,3,40,128]{3,2,1,0:T(8,128)S(1)} %get-tuple-element.22.mixed_ref, ...), custom_call_target="tpu_custom_call" | custom-call | tf_op jit(solution)/shard_map/basis/pallas_call | solution.py:555
  10.3 5.0 %collective-permute-start.2 = (f32[2,24,128]{2,1,0:T(8,128)S(1)}, f32[2,24,128]{2,1,0:T(8,128)S(1)}, u32[]{:S(2)}, u32[]{:S(2)}) collective-permute-start(f32[2,24,128]{2,1,0:T(8,128)S(1)} %get-tuple-element.28), channel_id=1, source_target_pairs={{0,2},{1,3},{2,0},{3,1},{4,6},{5,7},{6,4},{7,5},{8,10},{9,11},{10,... | collective-permute-start | bytes 73736 | tf_op jit(solution)/shard_map/ppermute | solution.py:579
  15.2 1.2 %collective-permute-done.2 = f32[2,24,128]{2,1,0:T(8,128)S(1)} collective-permute-done((f32[2,24,128]{2,1,0:T(8,128)S(1)}, f32[2,24,128]{2,1,0:T(8,128)S(1)}, u32[]{:S(2)}, u32[]{:S(2)}) %collective-permute-start.2) | collective-permute-done | bytes 24608 | tf_op jit(solution)/shard_map/ppermute | solution.py:579
  16.5 0.1 add_select_fusion.1
  16.5 2.4 %collective-permute-start.3 = (f32[2,24,128]{2,1,0:T(8,128)S(1)}, f32[2,24,128]{2,1,0:T(8,128)S(1)}, u32[]{:S(2)}, u32[]{:S(2)}) collective-permute-start(f32[2,24,128]{2,1,0:T(8,128)S(1)} %add_select_fusion.1), channel_id=1, source_target_pairs={{0,4},{1,5},{2,6},{3,7},{4,0},{5,1},{6,2},{7,3},{8,12},{9,13},{10,... | collective-permute-start | bytes 73736 | tf_op jit(solution)/shard_map/ppermute | solution.py:579
  18.9 0.0 copy-done
  18.9 0.1 copy.11
  19.0 1.1 %collective-permute-done.3 = f32[2,24,128]{2,1,0:T(8,128)S(1)} collective-permute-done((f32[2,24,128]{2,1,0:T(8,128)S(1)}, f32[2,24,128]{2,1,0:T(8,128)S(1)}, u32[]{:S(2)}, u32[]{:S(2)}) %collective-permute-start.3) | collective-permute-done | bytes 24608 | tf_op jit(solution)/shard_map/ppermute | solution.py:579
  20.1 0.1 add_select_fusion.ends_ref
  20.2 0.7 %collective-permute-start.4 = (f32[2,24,128]{2,1,0:T(8,128)S(1)}, f32[2,24,128]{2,1,0:T(8,128)S(1)}, u32[]{:S(2)}, u32[]{:S(2)}) collective-permute-start(f32[2,24,128]{2,1,0:T(8,128)S(1)} %add_select_fusion.ends_ref), channel_id=1, source_target_pairs={{0,1},{1,0},{2,3},{3,2},{4,5},{5,4},{6,7},{7,6},{8,9},{9,8},{10,11... | collective-permute-start | bytes 73736 | tf_op jit(solution)/shard_map/ppermute | solution.py:583
  20.9 0.0 copy-done.1
  20.9 2.5 %gates.1 = (f32[12,3,4,32,128]{4,3,2,1,0:T(8,128)}, f32[10,16,128]{2,1,0:T(8,128)S(1)}) custom-call(f32[2,24,128]{2,1,0:T(8,128)S(1)} %add_select_fusion.ends_ref, f32[24,128]{1,0:T(8,128)S(1)} %pad.14.par_ref, f32[4,24,32,128]{3,2,1,0:T(8,128)S(1)} %bitcast.2), custom_call_target="tpu_custom_call" | custom-call | flops 16777216 | bytes 8388608 | tf_op jit(solution)/shard_map/gates/pallas_call | solution.py:587
  23.4 0.0 collective-permute-done.4
  23.4 4.8 %collective-permute-start.5 = (f32[2,24,128]{2,1,0:T(8,128)S(1)}, f32[2,24,128]{2,1,0:T(8,128)S(1)}, u32[]{:S(2)}, u32[]{:S(2)}) collective-permute-start(f32[2,24,128]{2,1,0:T(8,128)S(1)} %add.38), channel_id=1, source_target_pairs={{0,8},{8,0},{1,9},{9,1},{2,10},{10,2},{3,11},{11,3},{4,12},{12,4},... | collective-permute-start | bytes 73736 | tf_op jit(solution)/shard_map/ppermute | solution.py:606
  28.3 1.1 %rest.1 = f32[12,3,4,32,128]{4,3,2,1,0:T(8,128)} custom-call(f32[10,16,128]{2,1,0:T(8,128)S(1)} %get-tuple-element.31.w_ref, f32[4,24,32,128]{3,2,1,0:T(8,128)S(1)} %bitcast.3, f32[12,3,4,32,128]{4,3,2,1,0:T(8,128)} %get-tuple-element.32.before_ref), custom_call_target="tpu_custom_call", output_to_operand_aliasing={{}: (2, {})} | custom-call | flops 4194304 | bytes 2097152 | tf_op jit(solution)/shard_map/rest/pallas_call | solution.py:607
  29.4 0.0 collective-permute-done.5
  29.4 0.7 %traces.1 = f32[12,3,256]{2,1,0:T(4,128)} custom-call(f32[10,16,128]{2,1,0:T(8,128)S(1)} %get-tuple-element.31.w_ref, f32[2,24,128]{2,1,0:T(8,128)S(1)} %add.39.sel_ref), custom_call_target="tpu_custom_call" | custom-call | tf_op jit(solution)/shard_map/traces/pallas_call | solution.py:624
  (5 shorter events, 0.0 us)
Async XLA Ops:
  0.6 18.3 %copy-start = (f32[12,8]{0,1:T(8,128)S(1)}, f32[12,8]{0,1:T(8,128)}, u32[]{:S(2)}) copy-start(f32[12,8]{0,1:T(8,128)} %param.8) | copy-start | bytes 1156
  0.6 20.3 %copy-start.1 = (f32[8]{0:T(128)S(1)}, f32[8]{0:T(128)}, u32[]{:S(2)}) copy-start(f32[8]{0:T(128)} %param.7) | copy-start | bytes 100
  1.9 6.4 %collective-permute-start = (f32[352,128]{1,0:T(8,128)S(1)}, f32[352,128]{1,0:T(8,128)S(1)}, u32[]{:S(2)}, u32[]{:S(2)}) collective-permute-start(f32[352,128]{1,0:T(8,128)S(1)} %get-tuple-element.25), channel_id=1, source_target_pairs={{0,1},{1,0},{2,3},{3,2},{4,5},{5,4},{6,7},{7,6},{8,9},{9,8},{10,11... | collective-permute-start | bytes 540680 | tf_op jit(solution)/shard_map/ppermute | solution.py:520
  4.0 4.3 %collective-permute-start.1 = (f32[352,128]{1,0:T(8,128)S(1)}, f32[352,128]{1,0:T(8,128)S(1)}, u32[]{:S(2)}, u32[]{:S(2)}) collective-permute-start(f32[352,128]{1,0:T(8,128)S(1)} %get-tuple-element.26), channel_id=1, source_target_pairs={{1,2},{3,4},{5,6},{2,1},{4,3},{6,5},{9,10},{11,12},{13,14},{10,9},... | collective-permute-start | bytes 540680 | tf_op jit(solution)/shard_map/ppermute | solution.py:519
  10.3 6.2 %collective-permute-start.2 = (f32[2,24,128]{2,1,0:T(8,128)S(1)}, f32[2,24,128]{2,1,0:T(8,128)S(1)}, u32[]{:S(2)}, u32[]{:S(2)}) collective-permute-start(f32[2,24,128]{2,1,0:T(8,128)S(1)} %get-tuple-element.28), channel_id=1, source_target_pairs={{0,2},{1,3},{2,0},{3,1},{4,6},{5,7},{6,4},{7,5},{8,10},{9,11},{10,... | collective-permute-start | bytes 73736 | tf_op jit(solution)/shard_map/ppermute | solution.py:579
  16.5 3.6 %collective-permute-start.3 = (f32[2,24,128]{2,1,0:T(8,128)S(1)}, f32[2,24,128]{2,1,0:T(8,128)S(1)}, u32[]{:S(2)}, u32[]{:S(2)}) collective-permute-start(f32[2,24,128]{2,1,0:T(8,128)S(1)} %add_select_fusion.1), channel_id=1, source_target_pairs={{0,4},{1,5},{2,6},{3,7},{4,0},{5,1},{6,2},{7,3},{8,12},{9,13},{10,... | collective-permute-start | bytes 73736 | tf_op jit(solution)/shard_map/ppermute | solution.py:579
  20.2 3.2 %collective-permute-start.4 = (f32[2,24,128]{2,1,0:T(8,128)S(1)}, f32[2,24,128]{2,1,0:T(8,128)S(1)}, u32[]{:S(2)}, u32[]{:S(2)}) collective-permute-start(f32[2,24,128]{2,1,0:T(8,128)S(1)} %add_select_fusion.ends_ref), channel_id=1, source_target_pairs={{0,1},{1,0},{2,3},{3,2},{4,5},{5,4},{6,7},{7,6},{8,9},{9,8},{10,11... | collective-permute-start | bytes 73736 | tf_op jit(solution)/shard_map/ppermute | solution.py:583
  23.4 6.0 %collective-permute-start.5 = (f32[2,24,128]{2,1,0:T(8,128)S(1)}, f32[2,24,128]{2,1,0:T(8,128)S(1)}, u32[]{:S(2)}, u32[]{:S(2)}) collective-permute-start(f32[2,24,128]{2,1,0:T(8,128)S(1)} %add.38), channel_id=1, source_target_pairs={{0,8},{8,0},{1,9},{9,1},{2,10},{10,2},{3,11},{11,3},{4,12},{12,4},... | collective-permute-start | bytes 73736 | tf_op jit(solution)/shard_map/ppermute | solution.py:606

commit v4 on v3

--- a/solution.py
+++ b/solution.py
@@ -14,7 +14,9 @@
 SIGMA = 3 * (1 + len(FIELDS))
 ENDS = SIGMA + 1
 SLOTS = ENDS + 2
-PICKS = 4
+GROUP = 4
+LATE = 24
+PICKS = 8
 TILE = 8
 VMEM = pl.BlockSpec(memory_space=pltpu.VMEM)
 SMEM = pl.BlockSpec(memory_space=pltpu.SMEM)
@@ -445,35 +447,43 @@
     return total
 
 
-def combine(w_ref, bas_ref, out_ref, gates, layer):
-    half = bas_ref.shape[2]
-    for top in range(0, half, TILE):
-        part = slice(top, top + TILE)
-        moved = bas_ref[layer, SIGMA, part, :]
-        fields = [bas_ref[layer, at, part, :] for at in range(SIGMA)]
-        for g in range(gates):
-            weight = lambda word: w_ref[word, g : g + 1, :]
-            scale = power_sum(weight, moved)
-            for c in range(3):
-                total = scale * fields[c]
-                for at, word in enumerate(FIELDS, 1):
-                    total = total + weight(word) * fields[at * 3 + c]
-                out_ref[g, c, 0, part, :] = total
-
-
-def gate_kernel(ends_ref, par_ref, bas_ref, out_ref, w_ref, *, poles):
-    gates = out_ref.shape[0]
-
-    @pl.when(pl.program_id(0) == 0)
-    def _():
-        weights(ends_ref, par_ref, w_ref, gates, poles)
-
-    combine(w_ref, bas_ref, out_ref, gates, pl.program_id(0))
-
-
-def rest_kernel(w_ref, bas_ref, before_ref, out_ref, *, early):
+def combine(w_ref, bas_ref, out_hbm, buffer, sems, blocks):
+    gates = out_hbm.shape[0]
+    copies = []
+    for at, (layer, begin, end) in enumerate(blocks):
+        for low in range(0, gates, GROUP):
+            some = range(low, min(low + GROUP, gates))
+            for top in range(begin, end, TILE):
+                part = slice(top, top + TILE)
+                moved = bas_ref[layer, SIGMA, part, :]
+                fields = [bas_ref[layer, row, part, :] for row in range(SIGMA)]
+                for g in some:
+                    weight = lambda word: w_ref[word, g : g + 1, :]
+                    scale = power_sum(weight, moved)
+                    for c in range(3):
+                        total = scale * fields[c]
+                        for row, word in enumerate(FIELDS, 1):
+                            total = total + weight(word) * fields[row * 3 + c]
+                        buffer[at, g, c, part, :] = total
+            rows = pl.ds(begin, end - begin)
+            for g in some:
+                copy = pltpu.make_async_copy(
+                    buffer.at[at, g, :, rows], out_hbm.at[g, :, layer, rows], sems.at[at, g]
+                )
+                copy.start()
+                copies.append(copy)
+    for copy in copies:
+        copy.wait()
+
+
+def gate_kernel(ends_ref, par_ref, bas_ref, out_hbm, w_ref, buffer, sems, *, poles, blocks):
+    weights(ends_ref, par_ref, w_ref, out_hbm.shape[0], poles)
+    combine(w_ref, bas_ref, out_hbm, buffer, sems, blocks)
+
+
+def rest_kernel(w_ref, bas_ref, before_ref, out_hbm, buffer, sems, *, blocks):
     del before_ref
-    combine(w_ref, bas_ref, out_ref, out_ref.shape[0], pl.program_id(0) + early)
+    combine(w_ref, bas_ref, out_hbm, buffer, sems, blocks)
 
 
 def trace_kernel(w_ref, sel_ref, out_ref):
@@ -582,21 +592,23 @@
     ends = sel
     other = lax.ppermute(sel, "space", [(i, i ^ 1) for i in range(size)])
 
-    early = layers - 1
+    cut = half - LATE
+    early = [(layer, 0, half) for layer in range(layers - 1)] + [(layers - 1, 0, cut)]
+    late = [(layers - 1, cut, half)]
     gated_shape = jax.ShapeDtypeStruct((gates, 3, layers, half, depth), f32)
+
+    def buffers(number):
+        return [
+            pltpu.VMEM((number, gates, 3, half, depth), f32),
+            pltpu.SemaphoreType.DMA((number, gates)),
+        ]
+
     gated, w = pl.pallas_call(
-        functools.partial(gate_kernel, poles=poles),
-        grid=(early,),
+        functools.partial(gate_kernel, poles=poles, blocks=early),
         out_shape=[gated_shape, jax.ShapeDtypeStruct((WORDS, 16, 128), f32)],
-        in_specs=[
-            VMEM,
-            VMEM,
-            VMEM,
-        ],
-        out_specs=[
-            pl.BlockSpec((gates, 3, 1, half, depth), lambda i: (0, 0, i, 0, 0)),
-            pl.BlockSpec((WORDS, 16, 128), lambda i: (0, 0, 0)),
-        ],
+        in_specs=[VMEM, VMEM, VMEM],
+        out_specs=[hbm, VMEM],
+        scratch_shapes=buffers(len(early)),
         compiler_params=PARAMS,
         cost_estimate=pl.CostEstimate(flops=2**24, bytes_accessed=2**23, transcendentals=0),
         name="gates",
@@ -605,15 +617,11 @@
     sel, w = lax.optimization_barrier((sel + other, w))
     other = lax.ppermute(sel, "pole", [(0, 1), (1, 0)])
     gated = pl.pallas_call(
-        functools.partial(rest_kernel, early=early),
-        grid=(layers - early,),
+        functools.partial(rest_kernel, blocks=late),
         out_shape=gated_shape,
-        in_specs=[
-            VMEM,
-            VMEM,
-            hbm,
-        ],
-        out_specs=pl.BlockSpec((gates, 3, 1, half, depth), lambda i: (0, 0, i + early, 0, 0)),
+        in_specs=[VMEM, VMEM, hbm],
+        out_specs=hbm,
+        scratch_shapes=buffers(len(late)),
         input_output_aliases={2: 0},
         compiler_params=PARAMS,
         cost_estimate=pl.CostEstimate(flops=2**22, bytes_accessed=2**21, transcendentals=0),

time: 30.4 us -> 30.1 us (level)
  Pallas kernels: 8.87 us -> 8.32 us
  transfers between devices with their start and end apart: 6 -> 6, of which waited for: 3 -> 3; matrix products, arithmetic and copies ran while one was open for 3% -> 3% of each run, Pallas kernels for 20% -> 19%
where the time goes in v4:
time: 30.1 us; the launch traced here: 29.8 us
  starting transfers between devices  15.9 us (53%)
  Pallas kernels  8.32 us (28%)
  waiting for transfers between devices  2.79 us (9%)
  other arithmetic  1.95 us (6%)
  between operations  0.76 us (3%)
    ppermute x2, starting transfers between devices, per_device(): other = lax.ppermute(sel, 'space', [(i, i ^ stride) for i in range(size)])  7.45 us
    ppermute x1, starting transfers between devices, per_device(): other = lax.ppermute(sel, 'pole', [(0, 1), (1, 0)])  5.06 us
    pallas_call x1, Pallas kernels, per_device(): pl.pallas_call(own_kernel, out_shape=[jax.ShapeDtypeStruct((count + 1,),...  2.45 us
    pallas_call x1, Pallas kernels, per_device(): pl.pallas_call(functools.partial(gate_kernel, poles=poles, blocks=early),...  2.36 us
    ppermute x2, waiting for transfers between devices, per_device(): other = lax.ppermute(sel, 'space', [(i, i ^ stride) for i in range(size)])  2.34 us
    ppermute x1, starting transfers between devices, per_device(): first = lax.ppermute(first, 'space', [(i, i ^ 1) for i in range(size)])  2.14 us
    pallas_call x1, Pallas kernels, per_device(): pl.pallas_call(basis_kernel, out_shape=[jax.ShapeDtypeStruct((layers * SL...  1.73 us
    mul x1, other arithmetic, per_device(): conductivity * jnp.pad(source_field, ((0, 1), (0, 0), (0, 0), (0, 0)), co...  1.08 us
  transfers between devices with their start and end apart: 6, of which 3 were waited for; matrix products, arithmetic and copies ran while one was open for 3% of the time, Pallas kernels for 19%

profile of v4, /device:TPU:1, one launch (start us, length us, event | category | flops | bytes accessed | tf_op | source)
XLA Modules:
  0.0 29.8 jit_solution(4052340169751098758)
XLA Ops:
  0.6 0.0 copy-start
  0.6 0.0 copy-start.1
  0.7 1.1 %pad_multiply_fusion.all_ref = f32[4,4,64,128]{3,2,1,0:T(8,128)S(1)} fusion(f32[3,4,64,128]{3,2,1,0:T(8,128)} %param.6, f32[4,64,128]{2,1,0:T(8,128)} %param.5), kind=kLoop, calls=%fused_computation | loop fusion | flops 131072 | bytes 1048576 | tf_op jit(solution)/shard_map/mul | solution.py:526
  1.7 0.1 send.1
  1.9 2.1 %collective-permute-start = (f32[352,128]{1,0:T(8,128)S(1)}, f32[352,128]{1,0:T(8,128)S(1)}, u32[]{:S(2)}, u32[]{:S(2)}) collective-permute-start(f32[352,128]{1,0:T(8,128)S(1)} %get-tuple-element.25), channel_id=1, source_target_pairs={{0,1},{1,0},{2,3},{3,2},{4,5},{5,4},{6,7},{7,6},{8,9},{9,8},{10,11... | collective-permute-start | bytes 540680 | tf_op jit(solution)/shard_map/ppermute | solution.py:530
  4.0 0.7 %collective-permute-start.1 = (f32[352,128]{1,0:T(8,128)S(1)}, f32[352,128]{1,0:T(8,128)S(1)}, u32[]{:S(2)}, u32[]{:S(2)}) collective-permute-start(f32[352,128]{1,0:T(8,128)S(1)} %get-tuple-element.26), channel_id=1, source_target_pairs={{1,2},{3,4},{5,6},{2,1},{4,3},{6,5},{9,10},{11,12},{13,14},{10,9},... | collective-permute-start | bytes 540680 | tf_op jit(solution)/shard_map/ppermute | solution.py:529
  4.7 0.7 %and_select_fusion.1.code_ref = s32[256]{0:T(256)S(1)} fusion(s32[256]{0:T(256)} %param.9, s32[]{:T(128)S(6)} %mul.23, s32[]{:T(128)S(6)} %mul.22), kind=kLoop, calls=%fused_computation.6 | loop fusion | flops 14336 | bytes 2056 | tf_op jit(solution)/shard_map/jit(_where)/select_n | solution.py:538
  5.4 2.4 %owned.1 = (s32[257]{0:T(512)S(1)}, f32[4,40,128]{2,1,0:T(8,128)S(1)}, f32[4,3,40,128]{3,2,1,0:T(8,128)S(1)}, f32[4,3,40,128]{3,2,1,0:T(8,128)S(1)}, f32[4,3,40,128]{3,2,1,0:T(8,128)S(1)}) custom-call(s32[256]{0:T(256)S(1)} %and_select_fusion.1.code_ref, f32[4,40,128]{2,1,0:T(8,128)S(1)} %get-tuple-element.19.cond_ref, ...), custom_call_target="tpu_custom_call" | custom-call | flops 8388608 | bytes 4194304 | tf_op jit(solution)/shard_map/owned/pallas_call | solution.py:545
  7.8 0.4 %collective-permute-done.first_ref = f32[352,128]{1,0:T(8,128)S(1)} collective-permute-done((f32[352,128]{1,0:T(8,128)S(1)}, f32[352,128]{1,0:T(8,128)S(1)}, u32[]{:S(2)}, u32[]{:S(2)}) %collective-permute-start) | collective-permute-done | bytes 180256 | tf_op jit(solution)/shard_map/ppermute | solution.py:530
  8.3 0.0 collective-permute-done.1.second_ref
  8.3 1.7 %basis.1 = (f32[3072,128]{1,0:T(8,128)S(1)}, f32[2,24,128]{2,1,0:T(8,128)S(1)}) custom-call(f32[4,3,40,128]{3,2,1,0:T(8,128)S(1)} %get-tuple-element.18.field_ref, f32[4,40,128]{2,1,0:T(8,128)S(1)} %get-tuple-element.20.sig_ref, f32[4,3,40,128]{3,2,1,0:T(8,128)S(1)} %get-tuple-element.21.one_ref, f32[4,3,40,128]{3,2,1,0:T(8,128)S(1)} %get-tuple-element.22.mixed_ref, ...), custom_call_target="tpu_custom_call" | custom-call | tf_op jit(solution)/shard_map/basis/pallas_call | solution.py:565
  10.0 5.0 %collective-permute-start.2 = (f32[2,24,128]{2,1,0:T(8,128)S(1)}, f32[2,24,128]{2,1,0:T(8,128)S(1)}, u32[]{:S(2)}, u32[]{:S(2)}) collective-permute-start(f32[2,24,128]{2,1,0:T(8,128)S(1)} %get-tuple-element.28), channel_id=1, source_target_pairs={{0,2},{1,3},{2,0},{3,1},{4,6},{5,7},{6,4},{7,5},{8,10},{9,11},{10,... | collective-permute-start | bytes 73736 | tf_op jit(solution)/shard_map/ppermute | solution.py:589
  15.0 1.2 %collective-permute-done.2 = f32[2,24,128]{2,1,0:T(8,128)S(1)} collective-permute-done((f32[2,24,128]{2,1,0:T(8,128)S(1)}, f32[2,24,128]{2,1,0:T(8,128)S(1)}, u32[]{:S(2)}, u32[]{:S(2)}) %collective-permute-start.2) | collective-permute-done | bytes 24608 | tf_op jit(solution)/shard_map/ppermute | solution.py:589
  16.2 0.1 add_select_fusion.1
  16.3 2.5 %collective-permute-start.3 = (f32[2,24,128]{2,1,0:T(8,128)S(1)}, f32[2,24,128]{2,1,0:T(8,128)S(1)}, u32[]{:S(2)}, u32[]{:S(2)}) collective-permute-start(f32[2,24,128]{2,1,0:T(8,128)S(1)} %add_select_fusion.1), channel_id=1, source_target_pairs={{0,4},{1,5},{2,6},{3,7},{4,0},{5,1},{6,2},{7,3},{8,12},{9,13},{10,... | collective-permute-start | bytes 73736 | tf_op jit(solution)/shard_map/ppermute | solution.py:589
  18.8 0.0 copy-done
  18.8 0.1 copy.11
  18.8 1.1 %collective-permute-done.3 = f32[2,24,128]{2,1,0:T(8,128)S(1)} collective-permute-done((f32[2,24,128]{2,1,0:T(8,128)S(1)}, f32[2,24,128]{2,1,0:T(8,128)S(1)}, u32[]{:S(2)}, u32[]{:S(2)}) %collective-permute-start.3) | collective-permute-done | bytes 24608 | tf_op jit(solution)/shard_map/ppermute | solution.py:589
  20.0 0.1 add_select_fusion.ends_ref
  20.1 0.6 %collective-permute-start.4 = (f32[2,24,128]{2,1,0:T(8,128)S(1)}, f32[2,24,128]{2,1,0:T(8,128)S(1)}, u32[]{:S(2)}, u32[]{:S(2)}) collective-permute-start(f32[2,24,128]{2,1,0:T(8,128)S(1)} %add_select_fusion.ends_ref), channel_id=1, source_target_pairs={{0,1},{1,0},{2,3},{3,2},{4,5},{5,4},{6,7},{7,6},{8,9},{9,8},{10,11... | collective-permute-start | bytes 73736 | tf_op jit(solution)/shard_map/ppermute | solution.py:593
  20.6 0.0 copy-done.1
  20.7 2.4 %gates.1 = (f32[12,3,4,32,128]{4,3,2,1,0:T(8,128)}, f32[10,16,128]{2,1,0:T(8,128)S(1)}) custom-call(f32[2,24,128]{2,1,0:T(8,128)S(1)} %add_select_fusion.ends_ref, f32[24,128]{1,0:T(8,128)S(1)} %pad.14.par_ref, f32[4,24,32,128]{3,2,1,0:T(8,128)S(1)} %bitcast.2), custom_call_target="tpu_custom_call" | custom-call | flops 16777216 | bytes 8388608 | tf_op jit(solution)/shard_map/gates/pallas_call | solution.py:606
  23.0 0.0 collective-permute-done.4
  23.1 5.1 %collective-permute-start.5 = (f32[2,24,128]{2,1,0:T(8,128)S(1)}, f32[2,24,128]{2,1,0:T(8,128)S(1)}, u32[]{:S(2)}, u32[]{:S(2)}) collective-permute-start(f32[2,24,128]{2,1,0:T(8,128)S(1)} %add.38), channel_id=1, source_target_pairs={{0,8},{8,0},{1,9},{9,1},{2,10},{10,2},{3,11},{11,3},{4,12},{12,4},... | collective-permute-start | bytes 73736 | tf_op jit(solution)/shard_map/ppermute | solution.py:618
  28.1 1.0 %rest.1 = f32[12,3,4,32,128]{4,3,2,1,0:T(8,128)} custom-call(f32[10,16,128]{2,1,0:T(8,128)S(1)} %get-tuple-element.31.w_ref, f32[4,24,32,128]{3,2,1,0:T(8,128)S(1)} %bitcast.3, f32[12,3,4,32,128]{4,3,2,1,0:T(8,128)} %get-tuple-element.32.before_ref), custom_call_target="tpu_custom_call", output_to_operand_aliasing={{}: (2, {})} | custom-call | flops 4194304 | bytes 2097152 | tf_op jit(solution)/shard_map/rest/pallas_call | solution.py:619
  29.1 0.0 collective-permute-done.5
  29.1 0.7 %traces.1 = f32[12,3,256]{2,1,0:T(4,128)} custom-call(f32[10,16,128]{2,1,0:T(8,128)S(1)} %get-tuple-element.31.w_ref, f32[2,24,128]{2,1,0:T(8,128)S(1)} %add.39.sel_ref), custom_call_target="tpu_custom_call" | custom-call | tf_op jit(solution)/shard_map/traces/pallas_call | solution.py:632
  (5 shorter events, 0.0 us)
Async XLA Ops:
  0.6 18.1 %copy-start = (f32[12,8]{0,1:T(8,128)S(1)}, f32[12,8]{0,1:T(8,128)}, u32[]{:S(2)}) copy-start(f32[12,8]{0,1:T(8,128)} %param.8) | copy-start | bytes 1156
  0.6 20.0 %copy-start.1 = (f32[8]{0:T(128)S(1)}, f32[8]{0:T(128)}, u32[]{:S(2)}) copy-start(f32[8]{0:T(128)} %param.7) | copy-start | bytes 100
  1.9 6.4 %collective-permute-start = (f32[352,128]{1,0:T(8,128)S(1)}, f32[352,128]{1,0:T(8,128)S(1)}, u32[]{:S(2)}, u32[]{:S(2)}) collective-permute-start(f32[352,128]{1,0:T(8,128)S(1)} %get-tuple-element.25), channel_id=1, source_target_pairs={{0,1},{1,0},{2,3},{3,2},{4,5},{5,4},{6,7},{7,6},{8,9},{9,8},{10,11... | collective-permute-start | bytes 540680 | tf_op jit(solution)/shard_map/ppermute | solution.py:530
  4.0 4.3 %collective-permute-start.1 = (f32[352,128]{1,0:T(8,128)S(1)}, f32[352,128]{1,0:T(8,128)S(1)}, u32[]{:S(2)}, u32[]{:S(2)}) collective-permute-start(f32[352,128]{1,0:T(8,128)S(1)} %get-tuple-element.26), channel_id=1, source_target_pairs={{1,2},{3,4},{5,6},{2,1},{4,3},{6,5},{9,10},{11,12},{13,14},{10,9},... | collective-permute-start | bytes 540680 | tf_op jit(solution)/shard_map/ppermute | solution.py:529
  10.0 6.2 %collective-permute-start.2 = (f32[2,24,128]{2,1,0:T(8,128)S(1)}, f32[2,24,128]{2,1,0:T(8,128)S(1)}, u32[]{:S(2)}, u32[]{:S(2)}) collective-permute-start(f32[2,24,128]{2,1,0:T(8,128)S(1)} %get-tuple-element.28), channel_id=1, source_target_pairs={{0,2},{1,3},{2,0},{3,1},{4,6},{5,7},{6,4},{7,5},{8,10},{9,11},{10,... | collective-permute-start | bytes 73736 | tf_op jit(solution)/shard_map/ppermute | solution.py:589
  16.3 3.7 %collective-permute-start.3 = (f32[2,24,128]{2,1,0:T(8,128)S(1)}, f32[2,24,128]{2,1,0:T(8,128)S(1)}, u32[]{:S(2)}, u32[]{:S(2)}) collective-permute-start(f32[2,24,128]{2,1,0:T(8,128)S(1)} %add_select_fusion.1), channel_id=1, source_target_pairs={{0,4},{1,5},{2,6},{3,7},{4,0},{5,1},{6,2},{7,3},{8,12},{9,13},{10,... | collective-permute-start | bytes 73736 | tf_op jit(solution)/shard_map/ppermute | solution.py:589
  20.1 3.0 %collective-permute-start.4 = (f32[2,24,128]{2,1,0:T(8,128)S(1)}, f32[2,24,128]{2,1,0:T(8,128)S(1)}, u32[]{:S(2)}, u32[]{:S(2)}) collective-permute-start(f32[2,24,128]{2,1,0:T(8,128)S(1)} %add_select_fusion.ends_ref), channel_id=1, source_target_pairs={{0,1},{1,0},{2,3},{3,2},{4,5},{5,4},{6,7},{7,6},{8,9},{9,8},{10,11... | collective-permute-start | bytes 73736 | tf_op jit(solution)/shard_map/ppermute | solution.py:593
  23.1 6.1 %collective-permute-start.5 = (f32[2,24,128]{2,1,0:T(8,128)S(1)}, f32[2,24,128]{2,1,0:T(8,128)S(1)}, u32[]{:S(2)}, u32[]{:S(2)}) collective-permute-start(f32[2,24,128]{2,1,0:T(8,128)S(1)} %add.38), channel_id=1, source_target_pairs={{0,8},{8,0},{1,9},{9,1},{2,10},{10,2},{3,11},{11,3},{4,12},{12,4},... | collective-permute-start | bytes 73736 | tf_op jit(solution)/shard_map/ppermute | solution.py:618

commit v5 on v4

--- a/solution.py
+++ b/solution.py
@@ -486,15 +486,16 @@
     combine(w_ref, bas_ref, out_hbm, buffer, sems, blocks)
 
 
-def trace_kernel(w_ref, sel_ref, out_ref):
+def trace_kernel(w_ref, one_ref, other_ref, out_ref):
     gates = out_ref.shape[0]
     weight = lambda word: w_ref[word, :gates, :]
-    for group in range(sel_ref.shape[0]):
-        scale = power_sum(weight, sel_ref[group, SIGMA : SIGMA + 1, :])
-        for c in range(3):
-            total = scale * sel_ref[group, c : c + 1, :]
+    for group in range(one_ref.shape[0]):
+        sel = one_ref[group] + other_ref[group]
+        scale = power_sum(weight, sel[SIGMA : SIGMA + 1])
+        for c in range(3):
+            total = scale * sel[c : c + 1]
             for at, word in enumerate(FIELDS, 1):
-                total = total + weight(word) * sel_ref[group, at * 3 + c : at * 3 + c + 1, :]
+                total = total + weight(word) * sel[at * 3 + c : at * 3 + c + 1]
             for g in range(gates):
                 out_ref[g, c : c + 1, group * 128 : (group + 1) * 128] = total[g : g + 1]
 
@@ -627,16 +628,14 @@
         cost_estimate=pl.CostEstimate(flops=2**22, bytes_accessed=2**21, transcendentals=0),
         name="rest",
     )(w, basis, gated)
-    sel = sel + other
-
     traces = pl.pallas_call(
         trace_kernel,
         out_shape=jax.ShapeDtypeStruct((gates, 3, count), f32),
-        in_specs=[VMEM, VMEM],
+        in_specs=[VMEM, VMEM, VMEM],
         out_specs=VMEM,
         compiler_params=PARAMS,
         name="traces",
-    )(w, sel)
+    )(w, sel, other)
     return gated, traces
 
 

time: 30.1 us -> 30.2 us (level)
  no operation moved by 1% of the time
where the time goes in v5:
time: 30.2 us; the launch traced here: 29.9 us
  starting transfers between devices  16.1 us (53%)
  Pallas kernels  8.26 us (27%)
  waiting for transfers between devices  2.79 us (9%)
  other arithmetic  1.95 us (6%)
  between operations  0.75 us (2%)
    ppermute x2, starting transfers between devices, per_device(): other = lax.ppermute(sel, 'space', [(i, i ^ stride) for i in range(size)])  7.44 us
    ppermute x1, starting transfers between devices, per_device(): other = lax.ppermute(sel, 'pole', [(0, 1), (1, 0)])  5.06 us
    pallas_call x1, Pallas kernels, per_device(): pl.pallas_call(own_kernel, out_shape=[jax.ShapeDtypeStruct((count + 1,),...  2.45 us
    ppermute x2, waiting for transfers between devices, per_device(): other = lax.ppermute(sel, 'space', [(i, i ^ stride) for i in range(size)])  2.34 us
    pallas_call x1, Pallas kernels, per_device(): pl.pallas_call(functools.partial(gate_kernel, poles=poles, blocks=early),...  2.3 us
    ppermute x1, starting transfers between devices, per_device(): first = lax.ppermute(first, 'space', [(i, i ^ 1) for i in range(size)])  2.14 us
    pallas_call x1, Pallas kernels, per_device(): pl.pallas_call(basis_kernel, out_shape=[jax.ShapeDtypeStruct((layers * SL...  1.73 us
    mul x1, other arithmetic, per_device(): conductivity * jnp.pad(source_field, ((0, 1), (0, 0), (0, 0), (0, 0)), co...  1.08 us
  transfers between devices with their start and end apart: 6, of which 3 were waited for; matrix products, arithmetic and copies ran while one was open for 3% of the time, Pallas kernels for 19%

profile of v5, /device:TPU:1, one launch (start us, length us, event | category | flops | bytes accessed | tf_op | source)
XLA Modules:
  0.0 29.9 jit_solution(17014893056370897330)
XLA Ops:
  0.6 0.0 copy-start
  0.6 0.0 copy-start.1
  0.7 1.1 %pad_multiply_fusion.all_ref = f32[4,4,64,128]{3,2,1,0:T(8,128)S(1)} fusion(f32[3,4,64,128]{3,2,1,0:T(8,128)} %param.6, f32[4,64,128]{2,1,0:T(8,128)} %param.5), kind=kLoop, calls=%fused_computation | loop fusion | flops 131072 | bytes 1048576 | tf_op jit(solution)/shard_map/mul | solution.py:527
  1.7 0.1 send.1
  1.9 2.1 %collective-permute-start = (f32[352,128]{1,0:T(8,128)S(1)}, f32[352,128]{1,0:T(8,128)S(1)}, u32[]{:S(2)}, u32[]{:S(2)}) collective-permute-start(f32[352,128]{1,0:T(8,128)S(1)} %get-tuple-element.25), channel_id=1, source_target_pairs={{0,1},{1,0},{2,3},{3,2},{4,5},{5,4},{6,7},{7,6},{8,9},{9,8},{10,11... | collective-permute-start | bytes 540680 | tf_op jit(solution)/shard_map/ppermute | solution.py:531
  4.0 0.7 %collective-permute-start.1 = (f32[352,128]{1,0:T(8,128)S(1)}, f32[352,128]{1,0:T(8,128)S(1)}, u32[]{:S(2)}, u32[]{:S(2)}) collective-permute-start(f32[352,128]{1,0:T(8,128)S(1)} %get-tuple-element.26), channel_id=1, source_target_pairs={{1,2},{3,4},{5,6},{2,1},{4,3},{6,5},{9,10},{11,12},{13,14},{10,9},... | collective-permute-start | bytes 540680 | tf_op jit(solution)/shard_map/ppermute | solution.py:530
  4.7 0.7 %and_select_fusion.1.code_ref = s32[256]{0:T(256)S(1)} fusion(s32[256]{0:T(256)} %param.9, s32[]{:T(128)S(6)} %mul.23, s32[]{:T(128)S(6)} %mul.22), kind=kLoop, calls=%fused_computation.6 | loop fusion | flops 14336 | bytes 2056 | tf_op jit(solution)/shard_map/jit(_where)/select_n | solution.py:539
  5.4 2.4 %owned.1 = (s32[257]{0:T(512)S(1)}, f32[4,40,128]{2,1,0:T(8,128)S(1)}, f32[4,3,40,128]{3,2,1,0:T(8,128)S(1)}, f32[4,3,40,128]{3,2,1,0:T(8,128)S(1)}, f32[4,3,40,128]{3,2,1,0:T(8,128)S(1)}) custom-call(s32[256]{0:T(256)S(1)} %and_select_fusion.1.code_ref, f32[4,40,128]{2,1,0:T(8,128)S(1)} %get-tuple-element.19.cond_ref, ...), custom_call_target="tpu_custom_call" | custom-call | flops 8388608 | bytes 4194304 | tf_op jit(solution)/shard_map/owned/pallas_call | solution.py:546
  7.8 0.4 %collective-permute-done.first_ref = f32[352,128]{1,0:T(8,128)S(1)} collective-permute-done((f32[352,128]{1,0:T(8,128)S(1)}, f32[352,128]{1,0:T(8,128)S(1)}, u32[]{:S(2)}, u32[]{:S(2)}) %collective-permute-start) | collective-permute-done | bytes 180256 | tf_op jit(solution)/shard_map/ppermute | solution.py:531
  8.3 0.0 collective-permute-done.1.second_ref
  8.3 1.7 %basis.1 = (f32[3072,128]{1,0:T(8,128)S(1)}, f32[2,24,128]{2,1,0:T(8,128)S(1)}) custom-call(f32[4,3,40,128]{3,2,1,0:T(8,128)S(1)} %get-tuple-element.18.field_ref, f32[4,40,128]{2,1,0:T(8,128)S(1)} %get-tuple-element.20.sig_ref, f32[4,3,40,128]{3,2,1,0:T(8,128)S(1)} %get-tuple-element.21.one_ref, f32[4,3,40,128]{3,2,1,0:T(8,128)S(1)} %get-tuple-element.22.mixed_ref, ...), custom_call_target="tpu_custom_call" | custom-call | tf_op jit(solution)/shard_map/basis/pallas_call | solution.py:566
  10.0 5.0 %collective-permute-start.2 = (f32[2,24,128]{2,1,0:T(8,128)S(1)}, f32[2,24,128]{2,1,0:T(8,128)S(1)}, u32[]{:S(2)}, u32[]{:S(2)}) collective-permute-start(f32[2,24,128]{2,1,0:T(8,128)S(1)} %get-tuple-element.28), channel_id=1, source_target_pairs={{0,2},{1,3},{2,0},{3,1},{4,6},{5,7},{6,4},{7,5},{8,10},{9,11},{10,... | collective-permute-start | bytes 73736 | tf_op jit(solution)/shard_map/ppermute | solution.py:590
  15.0 1.2 %collective-permute-done.2 = f32[2,24,128]{2,1,0:T(8,128)S(1)} collective-permute-done((f32[2,24,128]{2,1,0:T(8,128)S(1)}, f32[2,24,128]{2,1,0:T(8,128)S(1)}, u32[]{:S(2)}, u32[]{:S(2)}) %collective-permute-start.2) | collective-permute-done | bytes 24608 | tf_op jit(solution)/shard_map/ppermute | solution.py:590
  16.2 0.1 add_select_fusion.1
  16.3 2.5 %collective-permute-start.3 = (f32[2,24,128]{2,1,0:T(8,128)S(1)}, f32[2,24,128]{2,1,0:T(8,128)S(1)}, u32[]{:S(2)}, u32[]{:S(2)}) collective-permute-start(f32[2,24,128]{2,1,0:T(8,128)S(1)} %add_select_fusion.1), channel_id=1, source_target_pairs={{0,4},{1,5},{2,6},{3,7},{4,0},{5,1},{6,2},{7,3},{8,12},{9,13},{10,... | collective-permute-start | bytes 73736 | tf_op jit(solution)/shard_map/ppermute | solution.py:590
  18.8 0.0 copy-done
  18.8 0.1 copy.11
  18.8 1.1 %collective-permute-done.3 = f32[2,24,128]{2,1,0:T(8,128)S(1)} collective-permute-done((f32[2,24,128]{2,1,0:T(8,128)S(1)}, f32[2,24,128]{2,1,0:T(8,128)S(1)}, u32[]{:S(2)}, u32[]{:S(2)}) %collective-permute-start.3) | collective-permute-done | bytes 24608 | tf_op jit(solution)/shard_map/ppermute | solution.py:590
  20.0 0.1 add_select_fusion.ends_ref
  20.0 0.8 %collective-permute-start.4 = (f32[2,24,128]{2,1,0:T(8,128)S(1)}, f32[2,24,128]{2,1,0:T(8,128)S(1)}, u32[]{:S(2)}, u32[]{:S(2)}) collective-permute-start(f32[2,24,128]{2,1,0:T(8,128)S(1)} %add_select_fusion.ends_ref), channel_id=1, source_target_pairs={{0,1},{1,0},{2,3},{3,2},{4,5},{5,4},{6,7},{7,6},{8,9},{9,8},{10,11... | collective-permute-start | bytes 73736 | tf_op jit(solution)/shard_map/ppermute | solution.py:594
  20.8 0.0 copy-done.1
  20.8 2.3 %gates.1 = (f32[12,3,4,32,128]{4,3,2,1,0:T(8,128)}, f32[10,16,128]{2,1,0:T(8,128)S(1)}) custom-call(f32[2,24,128]{2,1,0:T(8,128)S(1)} %add_select_fusion.ends_ref, f32[24,128]{1,0:T(8,128)S(1)} %pad.14.par_ref, f32[4,24,32,128]{3,2,1,0:T(8,128)S(1)} %bitcast.2), custom_call_target="tpu_custom_call" | custom-call | flops 16777216 | bytes 8388608 | tf_op jit(solution)/shard_map/gates/pallas_call | solution.py:607
  23.1 0.0 collective-permute-done.4
  23.2 5.1 %collective-permute-start.5 = (f32[2,24,128]{2,1,0:T(8,128)S(1)}, f32[2,24,128]{2,1,0:T(8,128)S(1)}, u32[]{:S(2)}, u32[]{:S(2)}) collective-permute-start(f32[2,24,128]{2,1,0:T(8,128)S(1)} %add.35.one_ref), channel_id=1, source_target_pairs={{0,8},{8,0},{1,9},{9,1},{2,10},{10,2},{3,11},{11,3},{4,12},{12,4},... | collective-permute-start | bytes 73736 | tf_op jit(solution)/shard_map/ppermute | solution.py:619
  28.2 1.0 %rest.1 = f32[12,3,4,32,128]{4,3,2,1,0:T(8,128)} custom-call(f32[10,16,128]{2,1,0:T(8,128)S(1)} %get-tuple-element.31.w_ref, f32[4,24,32,128]{3,2,1,0:T(8,128)S(1)} %bitcast.3, f32[12,3,4,32,128]{4,3,2,1,0:T(8,128)} %get-tuple-element.32.before_ref), custom_call_target="tpu_custom_call", output_to_operand_aliasing={{}: (2, {})} | custom-call | flops 4194304 | bytes 2097152 | tf_op jit(solution)/shard_map/rest/pallas_call | solution.py:620
  29.2 0.0 collective-permute-done.5.other_ref
  29.2 0.7 %traces.1 = f32[12,3,256]{2,1,0:T(4,128)} custom-call(f32[10,16,128]{2,1,0:T(8,128)S(1)} %get-tuple-element.31.w_ref, f32[2,24,128]{2,1,0:T(8,128)S(1)} %add.35.one_ref, f32[2,24,128]{2,1,0:T(8,128)S(1)} %collective-permute-done.5.other_ref), custom_call_target="tpu_custom_call" | custom-call | tf_op jit(solution)/shard_map/traces/pallas_call | solution.py:631
  (4 shorter events, 0.0 us)
Async XLA Ops:
  0.6 18.1 %copy-start = (f32[12,8]{0,1:T(8,128)S(1)}, f32[12,8]{0,1:T(8,128)}, u32[]{:S(2)}) copy-start(f32[12,8]{0,1:T(8,128)} %param.8) | copy-start | bytes 1156
  0.6 20.2 %copy-start.1 = (f32[8]{0:T(128)S(1)}, f32[8]{0:T(128)}, u32[]{:S(2)}) copy-start(f32[8]{0:T(128)} %param.7) | copy-start | bytes 100
  1.9 6.4 %collective-permute-start = (f32[352,128]{1,0:T(8,128)S(1)}, f32[352,128]{1,0:T(8,128)S(1)}, u32[]{:S(2)}, u32[]{:S(2)}) collective-permute-start(f32[352,128]{1,0:T(8,128)S(1)} %get-tuple-element.25), channel_id=1, source_target_pairs={{0,1},{1,0},{2,3},{3,2},{4,5},{5,4},{6,7},{7,6},{8,9},{9,8},{10,11... | collective-permute-start | bytes 540680 | tf_op jit(solution)/shard_map/ppermute | solution.py:531
  4.0 4.3 %collective-permute-start.1 = (f32[352,128]{1,0:T(8,128)S(1)}, f32[352,128]{1,0:T(8,128)S(1)}, u32[]{:S(2)}, u32[]{:S(2)}) collective-permute-start(f32[352,128]{1,0:T(8,128)S(1)} %get-tuple-element.26), channel_id=1, source_target_pairs={{1,2},{3,4},{5,6},{2,1},{4,3},{6,5},{9,10},{11,12},{13,14},{10,9},... | collective-permute-start | bytes 540680 | tf_op jit(solution)/shard_map/ppermute | solution.py:530
  10.0 6.2 %collective-permute-start.2 = (f32[2,24,128]{2,1,0:T(8,128)S(1)}, f32[2,24,128]{2,1,0:T(8,128)S(1)}, u32[]{:S(2)}, u32[]{:S(2)}) collective-permute-start(f32[2,24,128]{2,1,0:T(8,128)S(1)} %get-tuple-element.28), channel_id=1, source_target_pairs={{0,2},{1,3},{2,0},{3,1},{4,6},{5,7},{6,4},{7,5},{8,10},{9,11},{10,... | collective-permute-start | bytes 73736 | tf_op jit(solution)/shard_map/ppermute | solution.py:590
  16.3 3.7 %collective-permute-start.3 = (f32[2,24,128]{2,1,0:T(8,128)S(1)}, f32[2,24,128]{2,1,0:T(8,128)S(1)}, u32[]{:S(2)}, u32[]{:S(2)}) collective-permute-start(f32[2,24,128]{2,1,0:T(8,128)S(1)} %add_select_fusion.1), channel_id=1, source_target_pairs={{0,4},{1,5},{2,6},{3,7},{4,0},{5,1},{6,2},{7,3},{8,12},{9,13},{10,... | collective-permute-start | bytes 73736 | tf_op jit(solution)/shard_map/ppermute | solution.py:590
  20.0 3.1 %collective-permute-start.4 = (f32[2,24,128]{2,1,0:T(8,128)S(1)}, f32[2,24,128]{2,1,0:T(8,128)S(1)}, u32[]{:S(2)}, u32[]{:S(2)}) collective-permute-start(f32[2,24,128]{2,1,0:T(8,128)S(1)} %add_select_fusion.ends_ref), channel_id=1, source_target_pairs={{0,1},{1,0},{2,3},{3,2},{4,5},{5,4},{6,7},{7,6},{8,9},{9,8},{10,11... | collective-permute-start | bytes 73736 | tf_op jit(solution)/shard_map/ppermute | solution.py:594
  23.2 6.1 %collective-permute-start.5 = (f32[2,24,128]{2,1,0:T(8,128)S(1)}, f32[2,24,128]{2,1,0:T(8,128)S(1)}, u32[]{:S(2)}, u32[]{:S(2)}) collective-permute-start(f32[2,24,128]{2,1,0:T(8,128)S(1)} %add.35.one_ref), channel_id=1, source_target_pairs={{0,8},{8,0},{1,9},{9,1},{2,10},{10,2},{3,11},{11,3},{4,12},{12,4},... | collective-permute-start | bytes 73736 | tf_op jit(solution)/shard_map/ppermute | solution.py:619

commit v6 on v5

--- a/solution.py
+++ b/solution.py
@@ -201,6 +201,16 @@
     apply(field_ref, one_ref)
     apply(t11, mixed_ref)
     apply(t22, twice_ref)
+    keep = part_keep(lax.axis_index("pole"))
+    half = reach - TILE
+    for layer in range(1, layers - 1):
+        for c in range(3):
+            one = one_ref[layer, c]
+            one = jnp.concatenate([one[:half], one[half:] * keep], axis=0)
+            one_ref[layer, c] = one
+            mixed = mixed_ref[layer, c]
+            mixed = jnp.concatenate([mixed[:half], mixed[half:] * keep], axis=0)
+            mixed_ref[layer, c] = mixed + sig_ref[layer] * one
 
     total = code_ref.shape[0]
 
@@ -269,6 +279,16 @@
 
         return get
 
+    def view(ref, own_ref, slot):
+        return (own_ref, slot - first) if first < slot < last else (ref, slot)
+
+    def mixed_reader(ref, own_ref):
+        def get(slot, which):
+            array, at = view(ref, own_ref, slot)
+            return [array[at, c] if c in which else None for c in range(3)]
+
+        return get
+
     def sums(get):
         def get_u(slot):
             if slot < 0:
@@ -314,14 +334,14 @@
 
     curl_curl(sums(get_b), get_b, [0, 1], put_10)
     curl_curl(sums(get_b), get_b, [last + 1, last + 2], put_10)
-    for slot in inner:
+    for slot in (first, last):
         put_10(slot, completed(one_ref, slot, get_b))
     get_11 = reader(t11)
     curl_curl(sums(get_11), get_11, [first - 1], put_21)
     curl_curl(sums(get_11), get_11, [last + 1], put_21)
-    for slot in inner:
+    for slot in (first, last):
         put_21(slot, completed(mixed_ref, slot, get_11))
-    get_10 = reader(t10)
+    get_10 = mixed_reader(t10, one_ref)
     curl_curl(sums(get_10), get_10, list(range(first - 1, last + 2)), put_20)
 
     def store(word, slot, c, value):
@@ -331,8 +351,10 @@
     for slot in inner:
         for c in range(3):
             store(0, slot, c, field_ref[slot - first, c, :half, :])
-            for word, ref in enumerate((t10, t20, t21), 1):
-                store(word, slot, c, ref[slot, c, :half, :])
+            for word, (ref, at) in enumerate(
+                (view(t10, one_ref, slot), (t20, slot), view(t21, mixed_ref, slot)), 1
+            ):
+                store(word, slot, c, ref[at, c, :half, :])
         base = ((slot - first) * SLOTS + SIGMA) * half
         bas_ref[base : base + half, :] = sig_ref[slot - first, :half, :]
 
@@ -342,20 +364,21 @@
                 value = out[c][:half]
                 if before is not None:
                     moved = sig_ref[slot - first, :half, :]
-                    value = value + moved * before[slot, c, :half, :]
+                    ref, at = before(slot)
+                    value = value + moved * ref[at, c, :half, :]
                 store(word, slot, c, value)
 
         return put
 
-    get_20, get_21 = reader(t20), reader(t21)
+    get_20, get_21 = reader(t20), mixed_reader(t21, mixed_ref)
     curl_curl(sums(get_20), get_20, inner, put_3(4, None))
-    curl_curl(sums(get_21), get_21, inner, put_3(5, t20))
+    curl_curl(sums(get_21), get_21, inner, put_3(5, lambda slot: (t20, slot)))
 
     def get_22(slot, which):
         return [sig[slot] * t11[slot, c] if c in which else None for c in range(3)]
 
     for slot in inner:
-        put_3(6, t21)(slot, completed(twice_ref, slot, get_22))
+        put_3(6, lambda slot: view(t21, mixed_ref, slot))(slot, completed(twice_ref, slot, get_22))
 
     groups = sel_ref.shape[0]
     lane = lax.broadcasted_iota(jnp.int32, (SLOTS, depth), 1)

time: 30.2 us -> 30 us (level)
  starting transfers between devices: 16.1 us -> 15.7 us
where the time goes in v6:
time: 30 us; the launch traced here: 29.7 us
  starting transfers between devices  15.7 us (52%)
  Pallas kernels  8.44 us (28%)
  waiting for transfers between devices  2.85 us (10%)
  other arithmetic  1.95 us (6%)
  between operations  0.75 us (2%)
    ppermute x2, starting transfers between devices, per_device(): other = lax.ppermute(sel, 'space', [(i, i ^ stride) for i in range(size)])  7.27 us
    ppermute x1, starting transfers between devices, per_device(): other = lax.ppermute(sel, 'pole', [(0, 1), (1, 0)])  4.89 us
    pallas_call x1, Pallas kernels, per_device(): pl.pallas_call(own_kernel, out_shape=[jax.ShapeDtypeStruct((count + 1,),...  2.45 us
    ppermute x2, waiting for transfers between devices, per_device(): other = lax.ppermute(sel, 'space', [(i, i ^ stride) for i in range(size)])  2.4 us
    pallas_call x1, Pallas kernels, per_device(): pl.pallas_call(functools.partial(gate_kernel, poles=poles, blocks=early),...  2.3 us
    ppermute x1, starting transfers between devices, per_device(): first = lax.ppermute(first, 'space', [(i, i ^ 1) for i in range(size)])  2.14 us
    pallas_call x1, Pallas kernels, per_device(): pl.pallas_call(basis_kernel, out_shape=[jax.ShapeDtypeStruct((layers * SL...  1.91 us
    mul x1, other arithmetic, per_device(): conductivity * jnp.pad(source_field, ((0, 1), (0, 0), (0, 0), (0, 0)), co...  1.08 us
  transfers between devices with their start and end apart: 6, of which 3 were waited for; matrix products, arithmetic and copies ran while one was open for 3% of the time, Pallas kernels for 19%

profile of v6, /device:TPU:1, one launch (start us, length us, event | category | flops | bytes accessed | tf_op | source)
XLA Modules:
  0.0 29.7 jit_solution(1298819037428568407)
XLA Ops:
  0.6 0.0 copy-start
  0.6 0.0 copy-start.1
  0.7 1.1 %pad_multiply_fusion.all_ref = f32[4,4,64,128]{3,2,1,0:T(8,128)S(1)} fusion(f32[3,4,64,128]{3,2,1,0:T(8,128)} %param.6, f32[4,64,128]{2,1,0:T(8,128)} %param.5), kind=kLoop, calls=%fused_computation | loop fusion | flops 131072 | bytes 1048576 | tf_op jit(solution)/shard_map/mul | solution.py:550
  1.7 0.1 send.1
  1.9 2.1 %collective-permute-start = (f32[352,128]{1,0:T(8,128)S(1)}, f32[352,128]{1,0:T(8,128)S(1)}, u32[]{:S(2)}, u32[]{:S(2)}) collective-permute-start(f32[352,128]{1,0:T(8,128)S(1)} %get-tuple-element.25), channel_id=1, source_target_pairs={{0,1},{1,0},{2,3},{3,2},{4,5},{5,4},{6,7},{7,6},{8,9},{9,8},{10,11... | collective-permute-start | bytes 540680 | tf_op jit(solution)/shard_map/ppermute | solution.py:554
  4.0 0.7 %collective-permute-start.1 = (f32[352,128]{1,0:T(8,128)S(1)}, f32[352,128]{1,0:T(8,128)S(1)}, u32[]{:S(2)}, u32[]{:S(2)}) collective-permute-start(f32[352,128]{1,0:T(8,128)S(1)} %get-tuple-element.26), channel_id=1, source_target_pairs={{1,2},{3,4},{5,6},{2,1},{4,3},{6,5},{9,10},{11,12},{13,14},{10,9},... | collective-permute-start | bytes 540680 | tf_op jit(solution)/shard_map/ppermute | solution.py:553
  4.7 0.7 %and_select_fusion.1.code_ref = s32[256]{0:T(256)S(1)} fusion(s32[256]{0:T(256)} %param.9, s32[]{:T(128)S(6)} %mul.23, s32[]{:T(128)S(6)} %mul.22), kind=kLoop, calls=%fused_computation.6 | loop fusion | flops 14336 | bytes 2056 | tf_op jit(solution)/shard_map/jit(_where)/select_n | solution.py:562
  5.4 2.4 %owned.1 = (s32[257]{0:T(512)S(1)}, f32[4,40,128]{2,1,0:T(8,128)S(1)}, f32[4,3,40,128]{3,2,1,0:T(8,128)S(1)}, f32[4,3,40,128]{3,2,1,0:T(8,128)S(1)}, f32[4,3,40,128]{3,2,1,0:T(8,128)S(1)}) custom-call(s32[256]{0:T(256)S(1)} %and_select_fusion.1.code_ref, f32[4,40,128]{2,1,0:T(8,128)S(1)} %get-tuple-element.19.cond_ref, ...), custom_call_target="tpu_custom_call" | custom-call | flops 8388608 | bytes 4194304 | tf_op jit(solution)/shard_map/owned/pallas_call | solution.py:569
  7.8 0.4 %collective-permute-done.first_ref = f32[352,128]{1,0:T(8,128)S(1)} collective-permute-done((f32[352,128]{1,0:T(8,128)S(1)}, f32[352,128]{1,0:T(8,128)S(1)}, u32[]{:S(2)}, u32[]{:S(2)}) %collective-permute-start) | collective-permute-done | bytes 180256 | tf_op jit(solution)/shard_map/ppermute | solution.py:554
  8.3 0.0 collective-permute-done.1.second_ref
  8.3 1.9 %basis.1 = (f32[3072,128]{1,0:T(8,128)S(1)}, f32[2,24,128]{2,1,0:T(8,128)S(1)}) custom-call(f32[4,3,40,128]{3,2,1,0:T(8,128)S(1)} %get-tuple-element.18.field_ref, f32[4,40,128]{2,1,0:T(8,128)S(1)} %get-tuple-element.20.sig_ref, f32[4,3,40,128]{3,2,1,0:T(8,128)S(1)} %get-tuple-element.21.one_ref, f32[4,3,40,128]{3,2,1,0:T(8,128)S(1)} %get-tuple-element.22.mixed_ref, ...), custom_call_target="tpu_custom_call" | custom-call | tf_op jit(solution)/shard_map/basis/pallas_call | solution.py:589
  10.2 5.0 %collective-permute-start.2 = (f32[2,24,128]{2,1,0:T(8,128)S(1)}, f32[2,24,128]{2,1,0:T(8,128)S(1)}, u32[]{:S(2)}, u32[]{:S(2)}) collective-permute-start(f32[2,24,128]{2,1,0:T(8,128)S(1)} %get-tuple-element.28), channel_id=1, source_target_pairs={{0,2},{1,3},{2,0},{3,1},{4,6},{5,7},{6,4},{7,5},{8,10},{9,11},{10,... | collective-permute-start | bytes 73736 | tf_op jit(solution)/shard_map/ppermute | solution.py:613
  15.2 1.2 %collective-permute-done.2 = f32[2,24,128]{2,1,0:T(8,128)S(1)} collective-permute-done((f32[2,24,128]{2,1,0:T(8,128)S(1)}, f32[2,24,128]{2,1,0:T(8,128)S(1)}, u32[]{:S(2)}, u32[]{:S(2)}) %collective-permute-start.2) | collective-permute-done | bytes 24608 | tf_op jit(solution)/shard_map/ppermute | solution.py:613
  16.4 0.1 add_select_fusion.1
  16.4 2.3 %collective-permute-start.3 = (f32[2,24,128]{2,1,0:T(8,128)S(1)}, f32[2,24,128]{2,1,0:T(8,128)S(1)}, u32[]{:S(2)}, u32[]{:S(2)}) collective-permute-start(f32[2,24,128]{2,1,0:T(8,128)S(1)} %add_select_fusion.1), channel_id=1, source_target_pairs={{0,4},{1,5},{2,6},{3,7},{4,0},{5,1},{6,2},{7,3},{8,12},{9,13},{10,... | collective-permute-start | bytes 73736 | tf_op jit(solution)/shard_map/ppermute | solution.py:613
  18.8 0.0 copy-done
  18.8 0.1 copy.11
  18.8 1.2 %collective-permute-done.3 = f32[2,24,128]{2,1,0:T(8,128)S(1)} collective-permute-done((f32[2,24,128]{2,1,0:T(8,128)S(1)}, f32[2,24,128]{2,1,0:T(8,128)S(1)}, u32[]{:S(2)}, u32[]{:S(2)}) %collective-permute-start.3) | collective-permute-done | bytes 24608 | tf_op jit(solution)/shard_map/ppermute | solution.py:613
  20.0 0.1 add_select_fusion.ends_ref
  20.1 0.7 %collective-permute-start.4 = (f32[2,24,128]{2,1,0:T(8,128)S(1)}, f32[2,24,128]{2,1,0:T(8,128)S(1)}, u32[]{:S(2)}, u32[]{:S(2)}) collective-permute-start(f32[2,24,128]{2,1,0:T(8,128)S(1)} %add_select_fusion.ends_ref), channel_id=1, source_target_pairs={{0,1},{1,0},{2,3},{3,2},{4,5},{5,4},{6,7},{7,6},{8,9},{9,8},{10,11... | collective-permute-start | bytes 73736 | tf_op jit(solution)/shard_map/ppermute | solution.py:617
  20.8 0.0 copy-done.1
  20.8 2.3 %gates.1 = (f32[12,3,4,32,128]{4,3,2,1,0:T(8,128)}, f32[10,16,128]{2,1,0:T(8,128)S(1)}) custom-call(f32[2,24,128]{2,1,0:T(8,128)S(1)} %add_select_fusion.ends_ref, f32[24,128]{1,0:T(8,128)S(1)} %pad.14.par_ref, f32[4,24,32,128]{3,2,1,0:T(8,128)S(1)} %bitcast.2), custom_call_target="tpu_custom_call" | custom-call | flops 16777216 | bytes 8388608 | tf_op jit(solution)/shard_map/gates/pallas_call | solution.py:630
  23.1 0.0 collective-permute-done.4
  23.2 4.9 %collective-permute-start.5 = (f32[2,24,128]{2,1,0:T(8,128)S(1)}, f32[2,24,128]{2,1,0:T(8,128)S(1)}, u32[]{:S(2)}, u32[]{:S(2)}) collective-permute-start(f32[2,24,128]{2,1,0:T(8,128)S(1)} %add.35.one_ref), channel_id=1, source_target_pairs={{0,8},{8,0},{1,9},{9,1},{2,10},{10,2},{3,11},{11,3},{4,12},{12,4},... | collective-permute-start | bytes 73736 | tf_op jit(solution)/shard_map/ppermute | solution.py:642
  28.1 1.0 %rest.1 = f32[12,3,4,32,128]{4,3,2,1,0:T(8,128)} custom-call(f32[10,16,128]{2,1,0:T(8,128)S(1)} %get-tuple-element.31.w_ref, f32[4,24,32,128]{3,2,1,0:T(8,128)S(1)} %bitcast.3, f32[12,3,4,32,128]{4,3,2,1,0:T(8,128)} %get-tuple-element.32.before_ref), custom_call_target="tpu_custom_call", output_to_operand_aliasing={{}: (2, {})} | custom-call | flops 4194304 | bytes 2097152 | tf_op jit(solution)/shard_map/rest/pallas_call | solution.py:643
  29.1 0.0 collective-permute-done.5.other_ref
  29.1 0.7 %traces.1 = f32[12,3,256]{2,1,0:T(4,128)} custom-call(f32[10,16,128]{2,1,0:T(8,128)S(1)} %get-tuple-element.31.w_ref, f32[2,24,128]{2,1,0:T(8,128)S(1)} %add.35.one_ref, f32[2,24,128]{2,1,0:T(8,128)S(1)} %collective-permute-done.5.other_ref), custom_call_target="tpu_custom_call" | custom-call | tf_op jit(solution)/shard_map/traces/pallas_call | solution.py:654
  (4 shorter events, 0.0 us)
Async XLA Ops:
  0.6 18.1 %copy-start = (f32[12,8]{0,1:T(8,128)S(1)}, f32[12,8]{0,1:T(8,128)}, u32[]{:S(2)}) copy-start(f32[12,8]{0,1:T(8,128)} %param.8) | copy-start | bytes 1156
  0.6 20.2 %copy-start.1 = (f32[8]{0:T(128)S(1)}, f32[8]{0:T(128)}, u32[]{:S(2)}) copy-start(f32[8]{0:T(128)} %param.7) | copy-start | bytes 100
  1.9 6.4 %collective-permute-start = (f32[352,128]{1,0:T(8,128)S(1)}, f32[352,128]{1,0:T(8,128)S(1)}, u32[]{:S(2)}, u32[]{:S(2)}) collective-permute-start(f32[352,128]{1,0:T(8,128)S(1)} %get-tuple-element.25), channel_id=1, source_target_pairs={{0,1},{1,0},{2,3},{3,2},{4,5},{5,4},{6,7},{7,6},{8,9},{9,8},{10,11... | collective-permute-start | bytes 540680 | tf_op jit(solution)/shard_map/ppermute | solution.py:554
  4.0 4.3 %collective-permute-start.1 = (f32[352,128]{1,0:T(8,128)S(1)}, f32[352,128]{1,0:T(8,128)S(1)}, u32[]{:S(2)}, u32[]{:S(2)}) collective-permute-start(f32[352,128]{1,0:T(8,128)S(1)} %get-tuple-element.26), channel_id=1, source_target_pairs={{1,2},{3,4},{5,6},{2,1},{4,3},{6,5},{9,10},{11,12},{13,14},{10,9},... | collective-permute-start | bytes 540680 | tf_op jit(solution)/shard_map/ppermute | solution.py:553
  10.2 6.2 %collective-permute-start.2 = (f32[2,24,128]{2,1,0:T(8,128)S(1)}, f32[2,24,128]{2,1,0:T(8,128)S(1)}, u32[]{:S(2)}, u32[]{:S(2)}) collective-permute-start(f32[2,24,128]{2,1,0:T(8,128)S(1)} %get-tuple-element.28), channel_id=1, source_target_pairs={{0,2},{1,3},{2,0},{3,1},{4,6},{5,7},{6,4},{7,5},{8,10},{9,11},{10,... | collective-permute-start | bytes 73736 | tf_op jit(solution)/shard_map/ppermute | solution.py:613
  16.4 3.6 %collective-permute-start.3 = (f32[2,24,128]{2,1,0:T(8,128)S(1)}, f32[2,24,128]{2,1,0:T(8,128)S(1)}, u32[]{:S(2)}, u32[]{:S(2)}) collective-permute-start(f32[2,24,128]{2,1,0:T(8,128)S(1)} %add_select_fusion.1), channel_id=1, source_target_pairs={{0,4},{1,5},{2,6},{3,7},{4,0},{5,1},{6,2},{7,3},{8,12},{9,13},{10,... | collective-permute-start | bytes 73736 | tf_op jit(solution)/shard_map/ppermute | solution.py:613
  20.1 3.0 %collective-permute-start.4 = (f32[2,24,128]{2,1,0:T(8,128)S(1)}, f32[2,24,128]{2,1,0:T(8,128)S(1)}, u32[]{:S(2)}, u32[]{:S(2)}) collective-permute-start(f32[2,24,128]{2,1,0:T(8,128)S(1)} %add_select_fusion.ends_ref), channel_id=1, source_target_pairs={{0,1},{1,0},{2,3},{3,2},{4,5},{5,4},{6,7},{7,6},{8,9},{9,8},{10,11... | collective-permute-start | bytes 73736 | tf_op jit(solution)/shard_map/ppermute | solution.py:617
  23.2 5.9 %collective-permute-start.5 = (f32[2,24,128]{2,1,0:T(8,128)S(1)}, f32[2,24,128]{2,1,0:T(8,128)S(1)}, u32[]{:S(2)}, u32[]{:S(2)}) collective-permute-start(f32[2,24,128]{2,1,0:T(8,128)S(1)} %add.35.one_ref), channel_id=1, source_target_pairs={{0,8},{8,0},{1,9},{9,1},{2,10},{10,2},{3,11},{11,3},{4,12},{12,4},... | collective-permute-start | bytes 73736 | tf_op jit(solution)/shard_map/ppermute | solution.py:642
